TPU v7x, 32 devices: a whole 2x2x4 slice. The times are simulated.
32 devices in a mesh: fsdp: 8 (over y, x, core), seq: 4 (over z).
Axes of the slice: x: 2, y: 2, z: 4, core: 2. Of those that a mesh axis runs over, the one named last changes fastest.
Arguments:
- tokens: bfloat16 [8, 1568, 768], P('fsdp', 'seq'), may hold values from -80 to 80
- norm_gain: bfloat16 [3, 768], P(None, 'fsdp'), may hold values from 0.5 to 1.5
- norm_bias: bfloat16 [3, 768], P(None, 'fsdp'), may hold values from -3 to 3
- attn_qkv: bfloat16 [2, 768, 2304], P(None, 'fsdp'), may hold values from -0.21875 to 0.21875
- attn_qv_bias: bfloat16 [2, 1536], P(None, 'fsdp'), may hold values from -3 to 3
- attn_out: bfloat16 [2, 768, 768], P(None, 'fsdp'), may hold values from -0.875 to 0.875
- attn_out_bias: bfloat16 [2, 768], P(None, 'fsdp'), may hold values from -2 to 2
- mlp_in: bfloat16 [768, 3072], P('fsdp'), may hold values from -0.21875 to 0.21875
- mlp_in_bias: bfloat16 [3072], P('fsdp'), may hold values from -3 to 3
- mlp_out: bfloat16 [3072, 768], P('fsdp'), may hold values from -0.15625 to 0.15625
- mlp_out_bias: bfloat16 [768], P('fsdp'), may hold values from -2 to 2
- threshold: float32 [2, 12], replicated, may hold values from 0.5 to 4
- cotangent: bfloat16 [8, 1568, 768], P('fsdp', 'seq'), may hold values from -6 to 6
Outputs:
- mixed: bfloat16 [8, 1568, 768], P('fsdp', 'seq')
- grad_tokens: float32 [8, 1568, 768], P('fsdp', 'seq')
- grad_norm_gain: float32 [3, 768], P(None, 'fsdp')
- grad_norm_bias: float32 [3, 768], P(None, 'fsdp')
- grad_attn_qkv: float32 [2, 768, 2304], P(None, 'fsdp')
- grad_attn_qv_bias: float32 [2, 1536], P(None, 'fsdp')
- grad_attn_out: float32 [2, 768, 768], P(None, 'fsdp')
- grad_attn_out_bias: float32 [2, 768], P(None, 'fsdp')
- grad_mlp_in: float32 [768, 3072], P('fsdp')
- grad_mlp_in_bias: float32 [3072], P('fsdp')
- grad_mlp_out: float32 [3072, 768], P('fsdp')
- grad_mlp_out_bias: float32 [768], P('fsdp')
- logit_max: float32 [2, 12], replicated
- clipped_qk: float32 [2, 768, 1536], P(None, 'fsdp')
All inputs are finite; a program needn't handle non-finite values.
Results may differ from a plain program's by a relative error of at most 0.02.
Values may be sent and summed in bfloat16 or wider, within the bound.
No kernel may reach another device: no remote copies, remote signals or barrier semaphores. Data moves between devices by JAX's collectives and lax.ppermute only.
A program may use at most 256 MiB of HBM per device.

v0:
```python
import jax
import jax.numpy as jnp
from jax import lax
from jax.sharding import PartitionSpec as P

H = 12
PATCHES = 196
HD = 64


EPSILON = 1e-06
NEGATIVE = -1e30


def layer_norm(rows_in, gain_row, shift_row):
    centre = jnp.mean(rows_in, axis=-1, keepdims=True)
    centred = rows_in - centre
    second = jnp.mean(centred * centred, axis=-1, keepdims=True)
    return centred * lax.rsqrt(second + EPSILON) * gain_row + shift_row


def exact_gelu(hidden):
    return jax.nn.gelu(hidden, approximate=False)


def rows_inner(left_side, right_side):
    return lax.dot_general(
        left_side, right_side, (((0,), (0,)), ((), ())), preferred_element_type=jnp.float32
    )


def times_transposed(left_side, right_side):
    return lax.dot_general(
        left_side, right_side, (((1,), (1,)), ((), ())), preferred_element_type=jnp.float32
    )


def arrange(section, temporal, head_count):
    clip_count = section.shape[0]
    shaped = section.reshape(clip_count, -1, PATCHES, head_count, HD)
    if temporal:
        shaped = jnp.swapaxes(shaped, 1, 2)
    return shaped.reshape(-1, shaped.shape[2], head_count, HD)


def restore(grouped, temporal, clip_count):
    head_count = grouped.shape[2]
    if temporal:
        shaped = jnp.swapaxes(grouped.reshape(clip_count, PATCHES, -1, head_count, HD), 1, 2)
    else:
        shaped = grouped.reshape(clip_count, -1, PATCHES, head_count, HD)
    return shaped.reshape(clip_count, -1, head_count * HD)


def core_forward(queries, key_heads, value_heads, scale_factor):
    scores = (
        jnp.einsum("gqhd,gkhd->ghqk", queries, key_heads, preferred_element_type=jnp.float32)
        * scale_factor
    )
    row_peak = jnp.max(scores, axis=-1, keepdims=True)
    expo_terms = jnp.exp(scores - row_peak)
    row_total = jnp.sum(expo_terms, axis=-1, keepdims=True)
    weights_soft = (expo_terms / row_total).astype(jnp.bfloat16)
    context = jnp.einsum(
        "ghqk,gkhd->gqhd", weights_soft, value_heads, preferred_element_type=jnp.float32
    )
    return (
        context.astype(jnp.bfloat16),
        row_peak + jnp.log(row_total),
        jnp.max(row_peak, axis=(0, 2, 3)),
    )


def core_backward(queries, key_heads, value_heads, log_total, grad_context, scale_factor):
    scores = (
        jnp.einsum("gqhd,gkhd->ghqk", queries, key_heads, preferred_element_type=jnp.float32)
        * scale_factor
    )
    weights_soft = jnp.exp(scores - log_total)
    grad_weights = jnp.einsum(
        "gqhd,gkhd->ghqk", grad_context, value_heads, preferred_element_type=jnp.float32
    )
    row_inner = jnp.sum(weights_soft * grad_weights, axis=-1, keepdims=True)
    grad_scores = (weights_soft * (grad_weights - row_inner)).astype(jnp.bfloat16)
    grad_queries = (
        jnp.einsum("ghqk,gkhd->gqhd", grad_scores, key_heads, preferred_element_type=jnp.float32)
        * scale_factor
    )
    grad_keys = (
        jnp.einsum("ghqk,gqhd->gkhd", grad_scores, queries, preferred_element_type=jnp.float32)
        * scale_factor
    )
    grad_values = jnp.einsum(
        "ghqk,gqhd->gkhd",
        weights_soft.astype(jnp.bfloat16),
        grad_context,
        preferred_element_type=jnp.float32,
    )
    return (
        grad_queries.astype(jnp.bfloat16),
        grad_keys.astype(jnp.bfloat16),
        grad_values.astype(jnp.bfloat16),
    )


def attention_forward(rows_in, clip_shape, params, temporal, scale_factor):
    gain_row, shift_row, qkv_weight, qv_shift, out_weight, out_shift = params
    clip_count, local_len, model_width = clip_shape
    normed, norm_pull = jax.vjp(layer_norm, rows_in, gain_row, shift_row)
    normed_low = normed.astype(jnp.bfloat16)
    shift_full = jnp.concatenate(
        [qv_shift[:model_width], jnp.zeros((model_width,), jnp.float32), qv_shift[model_width:]]
    )
    projected = (
        jnp.dot(normed_low, qkv_weight, preferred_element_type=jnp.float32) + shift_full
    ).astype(jnp.bfloat16)
    stacked = projected.reshape(clip_count, local_len, 3, model_width)
    stacked = lax.all_to_all(stacked, "seq", split_axis=3, concat_axis=1, tiled=True)
    head_count = stacked.shape[3] // HD
    queries = arrange(stacked[:, :, 0], temporal, head_count)
    key_heads = arrange(stacked[:, :, 1], temporal, head_count)
    value_heads = arrange(stacked[:, :, 2], temporal, head_count)
    context, log_total, peak_heads = core_forward(queries, key_heads, value_heads, scale_factor)
    joined = restore(context, temporal, clip_count)
    joined = lax.all_to_all(joined, "seq", split_axis=1, concat_axis=2, tiled=True)
    filler = jnp.full((H,), NEGATIVE, jnp.float32)
    peak_heads = lax.dynamic_update_slice(filler, peak_heads, (lax.axis_index("seq") * head_count,))
    context_rows = joined.reshape(clip_count * local_len, model_width)
    branch = jnp.dot(context_rows, out_weight, preferred_element_type=jnp.float32) + out_shift
    saved_state = (norm_pull, normed_low, stacked, log_total, context_rows)
    return (rows_in + branch, saved_state, peak_heads)


def attention_backward(
    grad_rows, clip_shape, saved_state, qkv_weight, out_weight, temporal, scale_factor
):
    norm_pull, normed_low, stacked, log_total, context_rows = saved_state
    clip_count, local_len, model_width = clip_shape
    grad_branch = grad_rows.astype(jnp.bfloat16)
    grad_out_weight = rows_inner(context_rows, grad_branch)
    grad_out_shift = jnp.sum(grad_branch, axis=0, dtype=jnp.float32)
    grad_context = (
        times_transposed(grad_branch, out_weight)
        .astype(jnp.bfloat16)
        .reshape(clip_count, local_len, model_width)
    )
    grad_context = lax.all_to_all(grad_context, "seq", split_axis=2, concat_axis=1, tiled=True)
    head_count = stacked.shape[3] // HD
    queries = arrange(stacked[:, :, 0], temporal, head_count)
    key_heads = arrange(stacked[:, :, 1], temporal, head_count)
    value_heads = arrange(stacked[:, :, 2], temporal, head_count)
    grad_queries, grad_keys, grad_values = core_backward(
        queries,
        key_heads,
        value_heads,
        log_total,
        arrange(grad_context, temporal, head_count),
        scale_factor,
    )
    grad_stack = jnp.stack(
        [
            restore(grad_queries, temporal, clip_count),
            restore(grad_keys, temporal, clip_count),
            restore(grad_values, temporal, clip_count),
        ],
        axis=2,
    )
    grad_stack = lax.all_to_all(grad_stack, "seq", split_axis=1, concat_axis=3, tiled=True)
    grad_proj = grad_stack.reshape(clip_count * local_len, 3 * model_width)
    grad_qkv_weight = rows_inner(normed_low, grad_proj)
    column_sums = jnp.sum(grad_proj, axis=0, dtype=jnp.float32)
    grad_qv_shift = jnp.concatenate([column_sums[:model_width], column_sums[2 * model_width :]])
    grad_normed = times_transposed(grad_proj, qkv_weight)
    grad_input, grad_gain, grad_shift = norm_pull(grad_normed)
    return (
        grad_rows + grad_input,
        (grad_gain, grad_shift, grad_qkv_weight, grad_qv_shift, grad_out_weight, grad_out_shift),
    )


def on_device(
    tokens,
    norm_gain,
    norm_bias,
    attn_qkv,
    attn_qv_bias,
    attn_out,
    attn_out_bias,
    mlp_in,
    mlp_in_bias,
    mlp_out,
    mlp_out_bias,
    threshold,
    cotangent,
):
    clip_shape = tokens.shape
    clip_count, local_len, model_width = clip_shape
    scale_factor = HD ** (-0.5)
    gathered = (
        lax.all_gather(norm_gain, "fsdp", axis=1, tiled=True),
        lax.all_gather(norm_bias, "fsdp", axis=1, tiled=True),
        lax.all_gather(attn_qkv, "fsdp", axis=1, tiled=True),
        lax.all_gather(attn_qv_bias, "fsdp", axis=1, tiled=True),
        lax.all_gather(attn_out, "fsdp", axis=1, tiled=True),
        lax.all_gather(attn_out_bias, "fsdp", axis=1, tiled=True),
        lax.all_gather(mlp_in, "fsdp", axis=0, tiled=True),
        lax.all_gather(mlp_in_bias, "fsdp", axis=0, tiled=True),
        lax.all_gather(mlp_out, "fsdp", axis=0, tiled=True),
        lax.all_gather(mlp_out_bias, "fsdp", axis=0, tiled=True),
    )
    gain_rows = gathered[0].astype(jnp.float32)
    shift_rows = gathered[1].astype(jnp.float32)
    qv_shifts = gathered[3].astype(jnp.float32)
    out_shifts = gathered[5].astype(jnp.float32)
    in_shift = gathered[7].astype(jnp.float32)
    back_shift = gathered[9].astype(jnp.float32)
    token_rows = tokens.astype(jnp.float32).reshape(clip_count * local_len, model_width)
    space_params = (
        gain_rows[0],
        shift_rows[0],
        gathered[2][0],
        qv_shifts[0],
        gathered[4][0],
        out_shifts[0],
    )
    space_rows, space_saved, space_peak = attention_forward(
        token_rows, clip_shape, space_params, False, scale_factor
    )
    time_params = (
        gain_rows[1],
        shift_rows[1],
        gathered[2][1],
        qv_shifts[1],
        gathered[4][1],
        out_shifts[1],
    )
    time_rows, time_saved, time_peak = attention_forward(
        space_rows, clip_shape, time_params, True, scale_factor
    )
    normed, norm_pull = jax.vjp(layer_norm, time_rows, gain_rows[2], shift_rows[2])
    normed_low = normed.astype(jnp.bfloat16)
    hidden = jnp.dot(normed_low, gathered[6], preferred_element_type=jnp.float32) + in_shift
    active, gelu_pull = jax.vjp(exact_gelu, hidden)
    active_low = active.astype(jnp.bfloat16)
    output_rows = time_rows + (
        jnp.dot(active_low, gathered[8], preferred_element_type=jnp.float32) + back_shift
    )
    peak_pair = jnp.stack([space_peak, time_peak])
    logit_max = lax.pmax(peak_pair, ("fsdp", "seq"))
    backward_set = (
        lax.all_gather(norm_gain, "fsdp", axis=1, tiled=True),
        lax.all_gather(norm_bias, "fsdp", axis=1, tiled=True),
        lax.all_gather(attn_qkv, "fsdp", axis=1, tiled=True),
        lax.all_gather(attn_qv_bias, "fsdp", axis=1, tiled=True),
        lax.all_gather(attn_out, "fsdp", axis=1, tiled=True),
        lax.all_gather(attn_out_bias, "fsdp", axis=1, tiled=True),
        lax.all_gather(mlp_in, "fsdp", axis=0, tiled=True),
        lax.all_gather(mlp_in_bias, "fsdp", axis=0, tiled=True),
        lax.all_gather(mlp_out, "fsdp", axis=0, tiled=True),
        lax.all_gather(mlp_out_bias, "fsdp", axis=0, tiled=True),
    )
    grad_low = cotangent.reshape(clip_count * local_len, model_width)
    grad_back_weight = rows_inner(active_low, grad_low)
    grad_back_shift = jnp.sum(grad_low, axis=0, dtype=jnp.float32)
    grad_active = times_transposed(grad_low, backward_set[8])
    (grad_hidden,) = gelu_pull(grad_active)
    grad_hidden_low = grad_hidden.astype(jnp.bfloat16)
    grad_in_weight = rows_inner(normed_low, grad_hidden_low)
    grad_in_shift = jnp.sum(grad_hidden_low, axis=0, dtype=jnp.float32)
    grad_normed = times_transposed(grad_hidden_low, backward_set[6])
    grad_middle, grad_gain_mlp, grad_shift_mlp = norm_pull(grad_normed)
    grad_middle = grad_low.astype(jnp.float32) + grad_middle
    grad_middle, time_grads = attention_backward(
        grad_middle,
        clip_shape,
        time_saved,
        backward_set[2][1],
        backward_set[4][1],
        True,
        scale_factor,
    )
    grad_first, space_grads = attention_backward(
        grad_middle,
        clip_shape,
        space_saved,
        backward_set[2][0],
        backward_set[4][0],
        False,
        scale_factor,
    )
    grad_gains = jnp.stack([space_grads[0], time_grads[0], grad_gain_mlp])
    grad_shifts = jnp.stack([space_grads[1], time_grads[1], grad_shift_mlp])
    grad_qkv = jnp.stack([space_grads[2], time_grads[2]])
    grad_qv = jnp.stack([space_grads[3], time_grads[3]])
    grad_outw = jnp.stack([space_grads[4], time_grads[4]])
    grad_outb = jnp.stack([space_grads[5], time_grads[5]])
    summed = (
        lax.psum_scatter(grad_gains, "fsdp", scatter_dimension=1, tiled=True),
        lax.psum_scatter(grad_shifts, "fsdp", scatter_dimension=1, tiled=True),
        lax.psum_scatter(grad_qkv, "fsdp", scatter_dimension=1, tiled=True),
        lax.psum_scatter(grad_qv, "fsdp", scatter_dimension=1, tiled=True),
        lax.psum_scatter(grad_outw, "fsdp", scatter_dimension=1, tiled=True),
        lax.psum_scatter(grad_outb, "fsdp", scatter_dimension=1, tiled=True),
        lax.psum_scatter(grad_in_weight, "fsdp", scatter_dimension=0, tiled=True),
        lax.psum_scatter(grad_in_shift, "fsdp", scatter_dimension=0, tiled=True),
        lax.psum_scatter(grad_back_weight, "fsdp", scatter_dimension=0, tiled=True),
        lax.psum_scatter(grad_back_shift, "fsdp", scatter_dimension=0, tiled=True),
    )
    totals = (
        lax.psum(summed[0].astype(jnp.bfloat16), "seq").astype(jnp.float32),
        lax.psum(summed[1].astype(jnp.bfloat16), "seq").astype(jnp.float32),
        lax.psum(summed[2].astype(jnp.bfloat16), "seq").astype(jnp.float32),
        lax.psum(summed[3].astype(jnp.bfloat16), "seq").astype(jnp.float32),
        lax.psum(summed[4].astype(jnp.bfloat16), "seq").astype(jnp.float32),
        lax.psum(summed[5].astype(jnp.bfloat16), "seq").astype(jnp.float32),
        lax.psum(summed[6].astype(jnp.bfloat16), "seq").astype(jnp.float32),
        lax.psum(summed[7].astype(jnp.bfloat16), "seq").astype(jnp.float32),
        lax.psum(summed[8].astype(jnp.bfloat16), "seq").astype(jnp.float32),
        lax.psum(summed[9].astype(jnp.bfloat16), "seq").astype(jnp.float32),
    )
    factor = threshold / jnp.maximum(logit_max, threshold)
    column_scale = jnp.repeat(jnp.sqrt(factor), HD, axis=1)
    own_weight = attn_qkv.astype(jnp.float32)
    clipped = jnp.concatenate(
        [
            own_weight[:, :, :model_width] * column_scale[:, None, :],
            own_weight[:, :, model_width : 2 * model_width] * column_scale[:, None, :],
        ],
        axis=2,
    )
    mixed = output_rows.reshape(clip_shape).astype(jnp.bfloat16)
    grad_tokens = grad_first.reshape(clip_shape)
    return (
        mixed,
        grad_tokens,
        totals[0],
        totals[1],
        totals[2],
        totals[3],
        totals[4],
        totals[5],
        totals[6],
        totals[7],
        totals[8],
        totals[9],
        logit_max,
        clipped,
    )


def solution(mesh):
    placed = (
        P("fsdp", "seq", None),
        P(None, "fsdp"),
        P(None, "fsdp"),
        P(None, "fsdp", None),
        P(None, "fsdp"),
        P(None, "fsdp", None),
        P(None, "fsdp"),
        P("fsdp", None),
        P("fsdp"),
        P("fsdp", None),
        P("fsdp"),
        P(),
        P("fsdp", "seq", None),
    )
    return jax.shard_map(
        on_device,
        mesh=mesh,
        in_specs=placed,
        out_specs=(
            P("fsdp", "seq", None),
            P("fsdp", "seq", None),
            P(None, "fsdp"),
            P(None, "fsdp"),
            P(None, "fsdp", None),
            P(None, "fsdp"),
            P(None, "fsdp", None),
            P(None, "fsdp"),
            P("fsdp", None),
            P("fsdp"),
            P("fsdp", None),
            P("fsdp"),
            P(),
            P(None, "fsdp", None),
        ),
        check_vma=False,
    )
```

profile of v0, /device:TPU:0, one launch (start us, length us, event | category | flops | bytes accessed | tf_op | source)
XLA Modules:
  0.0 1195.8 jit_solution(15585529323376642931)
XLA Ops:
  8.7 10.5 all-gather.2
  19.2 8.7 all-gather
  38.5 23.0 %all-gather.10.cloned.1.call-done = bf16[2,768,2304]{2,1,0:T(8,128)(2,1)} async-done(((bf16[2,96,2304]{2,1,0:T(8,128)(2,1)}), bf16[2,768,2304]{2,1,0:T(8,128)(2,1)}) %all-gather.10.cloned.1.call-update) | async-done | bytes 7077904 | tf_op jit(solution)/shard_map/all_gather | solution.py:202
  81.5 70.4 %all-to-all-done = bf16[1,392,3,768]{1,2,0,3:T(4,128)(2,1)S(1)} async-done(((bf16[1,392,3,768]{1,2,0,3:T(4,128)(2,1)}), bf16[1,392,3,768]{1,2,0,3:T(4,128)(2,1)S(1)}, u32[]{:S(2)}, u32[]{:S(2)}) %all-to-all-start) | async-done | bytes 1806368 | tf_op jit(solution)/shard_map/all_to_all | solution.py:118
  181.2 9.1 reduce.31
  195.4 9.1 all-gather.3
  242.1 69.5 %all-to-all-done.2 = bf16[1,392,3,768]{1,2,0,3:T(4,128)(2,1)S(1)} async-done(((bf16[1,392,3,768]{1,2,0,3:T(4,128)(2,1)}), bf16[1,392,3,768]{1,2,0,3:T(4,128)(2,1)S(1)}, u32[]{:S(2)}, u32[]{:S(2)}) %all-to-all-start.2) | async-done | bytes 1806368 | tf_op jit(solution)/shard_map/all_to_all | solution.py:118
  352.0 11.2 reduce.32
  369.8 8.8 all-gather.4
  406.2 16.0 %multiply_convert_fusion.1 = (bf16[392,3072]{1,0:T(8,128)(2,1)}, f32[392,3072]{1,0:T(8,128)}, f32[392,3072]{1,0:T(8,128)}) fusion(f32[3072]{0:T(1024)S(1)} %bitcast.329, bf16[768,3072]{1,0:T(8,128)(2,1)} %all-gather.14.cloned.1.call-done, f32[392,768]{1,0:T(8,128)} %copy-done.6, f32[768]{0:T(1024)S(1)} %get-tuple-element.31, ...), kind=kOutput, calls=%fused_computation.14 | convolution fusion | flops 1930672128 | bytes 17986624 | tf_op jit(solution)/shard_map/dot_general | solution.py:242
  458.4 14.6 %all-to-all-done.4 = bf16[4,2,37632]{2,1,0:T(2,128)(2,1)} async-done(((bf16[4,2,37632]{2,1,0:T(2,128)(2,1)}), bf16[4,2,37632]{2,1,0:T(2,128)(2,1)}, u32[]{:S(2)}, u32[]{:S(2)}) %all-to-all-start.4) | async-done | bytes 602144 | tf_op jit(solution)/shard_map/all_to_all | solution.py:147
  525.0 68.0 %all-to-all-done.5 = bf16[1,1568,3,192]{3,2,0,1:T(4,128)(2,1)S(1)} async-done(((bf16[1,1568,3,192]{3,2,0,1:T(4,128)(2,1)}), bf16[1,1568,3,192]{3,2,0,1:T(4,128)(2,1)S(1)}, u32[]{:S(2)}, u32[]{:S(2)}) %all-to-all-start.5) | async-done | bytes 1806368 | tf_op jit(solution)/shard_map/all_to_all | solution.py:168
  646.3 15.2 %all-to-all-done.6 = bf16[4,2,37632]{2,1,0:T(2,128)(2,1)S(1)} async-done(((bf16[4,2,37632]{2,1,0:T(2,128)(2,1)}), bf16[4,2,37632]{2,1,0:T(2,128)(2,1)S(1)}, u32[]{:S(2)}, u32[]{:S(2)}) %all-to-all-start.6) | async-done | bytes 602144 | tf_op jit(solution)/shard_map/all_to_all | solution.py:147
  704.7 63.9 %all-to-all-done.7 = bf16[1,1568,3,192]{3,2,0,1:T(4,128)(2,1)S(1)} async-done(((bf16[1,1568,3,192]{3,2,0,1:T(4,128)(2,1)}), bf16[1,1568,3,192]{3,2,0,1:T(4,128)(2,1)S(1)}, u32[]{:S(2)}, u32[]{:S(2)}) %all-to-all-start.7) | async-done | bytes 1806368 | tf_op jit(solution)/shard_map/all_to_all | solution.py:168
  785.4 11.6 pad_maximum_fusion
  811.3 15.4 %reduce-scatter.23.cloned.1.call-done = f32[384,768]{1,0:T(8,128)} async-done(((f32[3072,768]{1,0:T(8,128)}), f32[384,768]{1,0:T(8,128)}) %reduce-scatter.23.cloned.1.call-update) | async-done | bytes 1179664 | tf_op jit(solution)/shard_map/reduce_scatter | solution.py:306
  828.9 102.6 %reduce-scatter.17.cloned.1.call-done = f32[2,96,2304]{2,1,0:T(8,128)} async-done(((f32[2,768,2304]{2,1,0:T(8,128)}), f32[2,96,2304]{2,1,0:T(8,128)}) %reduce-scatter.17.cloned.1.call-update) | async-done | bytes 1769488 | tf_op jit(solution)/shard_map/reduce_scatter | solution.py:300
  939.4 12.7 %all-reduce = bf16[768]{0:T(1024)(128)(2,1)S(1)} all-reduce(bf16[768]{0:T(1024)(128)(2,1)S(1)} %dynamic-update-slice), channel_id=1, replica_groups=mesh['fsdp'=8,'seq'=4] {'fsdp'}, use_global_device_ids=true, to_apply=%add | all-reduce | flops 768 | bytes 3072
  958.4 39.5 %pmax.7 = f32[2,12]{1,0:T(2,128)S(1)} all-reduce(f32[2,12]{1,0:T(2,128)S(1)} %pad_maximum_fusion.13), channel_id=1, replica_groups=mesh['fsdp'=8,'seq'=4] {'fsdp','seq'}, use_global_device_ids=true, to_apply=%region_52.0 | all-reduce | flops 24 | bytes 192 | tf_op jit(solution)/shard_map/pmax | solution.py:249
  1000.6 23.1 %all-reduce.3 = (bf16[3072]{0:T(1024)(128)(2,1)S(1)}, bf16[768]{0:T(1024)(128)(2,1)S(1)}) all-reduce(f32[3072]{0:T(1024)S(1)} %get-tuple-element.98, f32[768]{0:T(1024)S(1)} %get-tuple-element.74), channel_id=9, replica_groups=mesh['fsdp'=8,'seq'=4] {'fsdp'}, use_global_device_ids=true, to_apply=%region_43.0.clone | all-reduce | flops 3840 | bytes 23040
  1027.1 16.6 %reduce-scatter.25.cloned.1.call-done = f32[96,3]{1,0:T(8,128)} async-done(((f32[768,3]{1,0:T(8,128)}), f32[96,3]{1,0:T(8,128)}) %reduce-scatter.25.cloned.1.call-update) | async-done | bytes 1168
  1044.6 38.0 %reduce-scatter.29.cloned.1.call-done = f32[192,2]{1,0:T(8,128)} async-done(((f32[1536,2]{1,0:T(8,128)}), f32[192,2]{1,0:T(8,128)}) %reduce-scatter.29.cloned.1.call-update) | async-done | bytes 1552
  1083.6 12.0 %all-reduce.4 = (bf16[3,96]{1,0:T(4,128)(2,1)S(1)}, bf16[3,96]{1,0:T(4,128)(2,1)S(1)}, bf16[2,192]{1,0:T(2,128)(2,1)S(1)}, bf16[2,96]{1,0:T(2,128)(2,1)S(1)}, bf...) all-reduce(bf16[3,96]{1,0:T(4,128)(2,1)S(1)} %copy.290, ...), channel_id=1, replica_groups=mesh['fsdp'=8,'seq'=4] {'seq'}, use_global_device_ids=true, to_apply=%region_22.0 | all-reduce | flops 1632 | bytes 6528 | tf_op jit(solution)/shard_map/psum | solution.py:310
  1099.0 84.3 %all-reduce.8.cloned.1.call-done = (bf16[2,96,2304]{2,1,0:T(8,128)(2,1)}, bf16[2,96,768]{2,1,0:T(8,128)(2,1)}, bf16[96,3072]{1,0:T(8,128)(2,1)}, bf16[384,768]{1,0:T(8,128)(2,1)}) async-done(((bf16[2,96,2304]{2,1,0:T(8,128)(2,1)}, bf16[2,96,768]{2,1,0:T(8,128)(2,1)}, bf16[96,3072]{1,0:T(8,128)(2,1)}, bf16[384,768]{1,0:T(8,128)(2,1)}), (bf16[2,96,2304]{2,1,0:T(8,128)(2,1)}, bf16[2,96,768]{2,1,0:T(8,128)(2,1)}, ...) | async-done | bytes 2359312 | tf_op jit(solution)/shard_map/psum | solution.py:312
  (388 shorter events, 424.5 us)
Async XLA Ops:
  7.2 30.4 %copy-start.14 = (bf16[1,392,768]{2,1,0:T(8,128)(2,1)S(1)}, bf16[1,392,768]{2,1,0:T(8,128)(2,1)}, u32[]{:S(2)}) copy-start(bf16[1,392,768]{2,1,0:T(8,128)(2,1)} %param.13) | copy-start | bytes 1806340
  7.2 54.4 %all-gather.10.cloned.1.call-start = ((), (), s32[]{:S(2)}) async-start(), calls=%async_computation.16 | async-start | bytes 7962624 | tf_op jit(solution)/shard_map/all_gather | solution.py:202
  7.9 212.1 %all-gather.12.cloned.1.call-start = ((), (), s32[]{:S(2)}) async-start(), calls=%async_computation.17 | async-start | bytes 2654208 | tf_op jit(solution)/shard_map/all_gather | solution.py:204
  36.4 186.2 %copy-start.55 = (f32[768]{0:T(1024)}, f32[768]{0:T(1024)S(1)}, u32[]{:S(2)}) copy-start(f32[768]{0:T(1024)S(1)} %get-tuple-element.32) | copy-start | bytes 9220
  76.2 75.7 %all-to-all-start = ((bf16[1,392,3,768]{1,2,0,3:T(4,128)(2,1)}), bf16[1,392,3,768]{1,2,0,3:T(4,128)(2,1)S(1)}, u32[]{:S(2)}, u32[]{:S(2)}) async-start(bf16[1,392,3,768]{1,2,0,3:T(4,128)(2,1)} %copy.230), calls=%async_computation | async-start | bytes 6291456 | tf_op jit(solution)/shard_map/all_to_all | solution.py:118
  80.8 325.4 %all-gather.14.cloned.1.call-start = ((), (), s32[]{:S(2)}) async-start(), calls=%async_computation.18 | async-start | bytes 5308416 | tf_op jit(solution)/shard_map/all_gather | solution.py:206
  191.9 19.2 %all-to-all-start.1 = ((bf16[4,2,37632]{2,1,0:T(2,128)(2,1)}), bf16[4,2,37632]{2,1,0:T(2,128)(2,1)S(1)}, u32[]{:S(2)}, u32[]{:S(2)}) async-start(bf16[4,2,37632]{2,1,0:T(2,128)(2,1)} %reshape.370), calls=%async_computation.1 | async-start | bytes 1204224 | tf_op jit(solution)/shard_map/all_to_all | solution.py:125
  237.8 73.8 %all-to-all-start.2 = ((bf16[1,392,3,768]{1,2,0,3:T(4,128)(2,1)}), bf16[1,392,3,768]{1,2,0,3:T(4,128)(2,1)S(1)}, u32[]{:S(2)}, u32[]{:S(2)}) async-start(bf16[1,392,3,768]{1,2,0,3:T(4,128)(2,1)} %copy.242), calls=%async_computation.2 | async-start | bytes 6291456 | tf_op jit(solution)/shard_map/all_to_all | solution.py:118
  241.5 180.7 %all-gather.16.cloned.1.call-start = ((), (), s32[]{:S(2)}) async-start(), calls=%async_computation.19 | async-start | bytes 5308416 | tf_op jit(solution)/shard_map/all_gather | solution.py:208
  366.3 19.1 %all-to-all-start.3 = ((bf16[4,2,37632]{2,1,0:T(2,128)(2,1)}), bf16[4,2,37632]{2,1,0:T(2,128)(2,1)S(1)}, u32[]{:S(2)}, u32[]{:S(2)}) async-start(bf16[4,2,37632]{2,1,0:T(2,128)(2,1)} %reshape.372), calls=%async_computation.3 | async-start | bytes 1204224 | tf_op jit(solution)/shard_map/all_to_all | solution.py:125
  452.9 20.0 %all-to-all-start.4 = ((bf16[4,2,37632]{2,1,0:T(2,128)(2,1)}), bf16[4,2,37632]{2,1,0:T(2,128)(2,1)}, u32[]{:S(2)}, u32[]{:S(2)}) async-start(bf16[4,2,37632]{2,1,0:T(2,128)(2,1)} %reshape.374), calls=%async_computation.4 | async-start | bytes 1204224 | tf_op jit(solution)/shard_map/all_to_all | solution.py:147
  517.8 75.3 %all-to-all-start.5 = ((bf16[1,1568,3,192]{3,2,0,1:T(4,128)(2,1)}), bf16[1,1568,3,192]{3,2,0,1:T(4,128)(2,1)S(1)}, u32[]{:S(2)}, u32[]{:S(2)}) async-start(bf16[1,1568,3,192]{3,2,0,1:T(4,128)(2,1)} %copy.261), calls=%async_computation.5 | async-start | bytes 6422528 | tf_op jit(solution)/shard_map/all_to_all | solution.py:168
  521.5 285.8 %reduce-scatter.19.cloned.1.call-start = ((), (), s32[]{:S(2)}) async-start(), calls=%async_computation.21 | async-start | bytes 5308416 | tf_op jit(solution)/shard_map/reduce_scatter | solution.py:302
  613.9 195.2 %reduce-scatter.21.cloned.1.call-start = ((), (), s32[]{:S(2)}) async-start(), calls=%async_computation.22 | async-start | bytes 10616832 | tf_op jit(solution)/shard_map/reduce_scatter | solution.py:304
  623.0 203.7 %reduce-scatter.23.cloned.1.call-start = ((), (), s32[]{:S(2)}) async-start(), calls=%async_computation.23 | async-start | bytes 10616832 | tf_op jit(solution)/shard_map/reduce_scatter | solution.py:306
  642.6 18.9 %all-to-all-start.6 = ((bf16[4,2,37632]{2,1,0:T(2,128)(2,1)}), bf16[4,2,37632]{2,1,0:T(2,128)(2,1)S(1)}, u32[]{:S(2)}, u32[]{:S(2)}) async-start(bf16[4,2,37632]{2,1,0:T(2,128)(2,1)} %reshape.376), calls=%async_computation.6 | async-start | bytes 1204224 | tf_op jit(solution)/shard_map/all_to_all | solution.py:147
  693.3 75.2 %all-to-all-start.7 = ((bf16[1,1568,3,192]{3,2,0,1:T(4,128)(2,1)}), bf16[1,1568,3,192]{3,2,0,1:T(4,128)(2,1)S(1)}, u32[]{:S(2)}, u32[]{:S(2)}) async-start(bf16[1,1568,3,192]{3,2,0,1:T(4,128)(2,1)} %copy.277), calls=%async_computation.7 | async-start | bytes 6422528 | tf_op jit(solution)/shard_map/all_to_all | solution.py:168
  697.4 234.1 %reduce-scatter.17.cloned.1.call-start = ((), (), s32[]{:S(2)}) async-start(), calls=%async_computation.20 | async-start | bytes 15925248 | tf_op jit(solution)/shard_map/reduce_scatter | solution.py:300
  797.0 226.8 %reduce-scatter.31.cloned.1.call-start = ((), (), s32[]{:S(2)}) async-start(), calls=%async_computation.27 | async-start | bytes 442368
  798.3 227.9 %reduce-scatter.27.cloned.1.call-start = ((), (), s32[]{:S(2)}) async-start(), calls=%async_computation.25 | async-start | bytes 442368
  804.8 238.9 %reduce-scatter.25.cloned.1.call-start = ((), (), s32[]{:S(2)}) async-start(), calls=%async_computation.24 | async-start | bytes 442368
  805.9 276.7 %reduce-scatter.29.cloned.1.call-start = ((), (), s32[]{:S(2)}) async-start(), calls=%async_computation.26 | async-start | bytes 884736
  807.2 376.1 %all-reduce.8.cloned.1.call-start = ((), (), s32[]{:S(2)}) async-start(), calls=%async_computation.28 | async-start | bytes 4718592 | tf_op jit(solution)/shard_map/psum | solution.py:312
  952.4 45.4 %copy-start.59 = (f32[2,12]{1,0:T(2,128)S(1)}, f32[2,12]{1,0:T(2,128)}, u32[]{:S(2)}) copy-start(f32[2,12]{1,0:T(2,128)} %param.24) | copy-start | bytes 292
  (64 other events, 398.1 us)
Sparse Core Ops, SparseCore 0:
  9.9 51.5 all-gather.9
  63.5 29.0 all-gather.11
  94.4 38.9 all-gather.13
  244.0 39.3 all-gather.15
  614.0 51.9 reduce-scatter.18
  669.8 76.4 reduce-scatter.20
  750.2 76.4 reduce-scatter.22
  830.7 100.7 reduce-scatter.16
  935.4 33.8 reduce-scatter.30
  972.5 33.9 reduce-scatter.26
  1009.9 33.8 reduce-scatter.24
  1047.6 34.9 reduce-scatter.28
  1086.6 96.6 all-reduce.7
where the time goes:
time: 1200 us
  waiting for transfers between devices  597 us (50%)
  local copies, waits for them, and re-layouts  202 us (17%)
  blocking collectives  132 us (11%)
  matrix products  119 us (10%)
  other arithmetic  95.1 us (8%)
  starting transfers between devices  32.2 us (3%)
  between operations  17.5 us (1%)
    all_to_all x2, waiting for transfers between devices, attention_forward(): lax.all_to_all(stacked, 'seq', split_axis=3, concat_axis=1, tiled=True)  140 us
    all_to_all x2, waiting for transfers between devices, attention_backward(): lax.all_to_all(grad_stack, 'seq', split_axis=1, concat_axis=3, tiled=True)  132 us
    reduce_scatter x1, waiting for transfers between devices, on_device(): lax.psum_scatter(grad_qkv, 'fsdp', scatter_dimension=1, tiled=True)  103 us
    psum x1, waiting for transfers between devices, on_device(): lax.psum(summed[2].astype(jnp.bfloat16), 'seq').astype(jnp.float32)  84.3 us
    unnamed x17, waiting for transfers between devices  57.2 us
    unnamed x157, local copies, waits for them, and re-layouts  40.6 us
    pmax x1, blocking collectives, on_device(): logit_max = lax.pmax(peak_pair, ('fsdp', 'seq'))  39.5 us
    unnamed x2, blocking collectives  35.8 us
  transfers between devices with their start and end apart: 21, of which 14 were waited for; matrix products, arithmetic and copies ran while one was open for 25% of the time, Pallas kernels for 0%

commit v1 on v0

v1 whole, which is shorter than its diff:
```python
import functools

import jax
import jax.numpy as jnp
from jax import lax
from jax.experimental import pallas as pl
from jax.experimental.pallas import tpu as pltpu
from jax.sharding import PartitionSpec as P

H = 12
PATCHES = 196
HD = 64
D = 768
PAIRS = H // 2
CHUNK = 208
BLOCKS = 2
ROWS = BLOCKS * CHUNK
FF_BLOCK = 768
EPSILON = 1e-06
NEGATIVE = -1e30
SCALE = HD ** (-0.5)
VMEM_LIMIT = 58 * 1024 * 1024
BF = jnp.bfloat16
F32 = jnp.float32


def mm(a, b):
    return lax.dot_general(a, b, (((1,), (0,)), ((), ())), preferred_element_type=F32)


def mm_nt(a, b):
    return lax.dot_general(a, b, (((1,), (1,)), ((), ())), preferred_element_type=F32)


def mm_tn(a, b):
    return lax.dot_general(a, b, (((0,), (0,)), ((), ())), preferred_element_type=F32)


def row_stats(rows):
    centre = jnp.mean(rows, axis=-1, keepdims=True)
    centred = rows - centre
    second = jnp.mean(centred * centred, axis=-1, keepdims=True)
    inverse = lax.rsqrt(second + EPSILON)
    return centred * inverse, inverse


def norm_backward(grad, unit, inverse, gain):
    weighted = grad * gain
    first = jnp.mean(weighted, axis=-1, keepdims=True)
    second = jnp.mean(weighted * unit, axis=-1, keepdims=True)
    return (weighted - first - unit * second) * inverse


def column_sum(values):
    return jnp.sum(values.astype(F32), axis=0, keepdims=True)


def masks(temporal, block, frames):
    row = lax.broadcasted_iota(jnp.int32, (2 * CHUNK, CHUNK), 0)
    col = lax.broadcasted_iota(jnp.int32, (2 * CHUNK, CHUNK), 1)
    if temporal:
        row = jnp.where(row >= CHUNK, row - CHUNK, row)
        allowed = (row // frames) == (col // frames)
    else:
        allowed = col < PATCHES
    return allowed


def lower_lanes(rows):
    return lax.broadcasted_iota(jnp.int32, (rows, 2 * HD), 1) < HD


def split_heads(pair, scale=None):
    low_half = lower_lanes(pair.shape[0])
    if scale is not None:
        pair = pair * jnp.asarray(scale, pair.dtype)
    zero = jnp.zeros_like(pair)
    return jnp.where(low_half, pair, zero), jnp.where(low_half, zero, pair)


def attend_forward(proj_ref, ctx_ref, soft_ref, peak_ref, temporal, frames, valid):
    lane = lax.broadcasted_iota(jnp.int32, (8, 128), 1)
    peaks = jnp.full((8, 128), NEGATIVE, F32)
    for block in range(BLOCKS):
        allowed = masks(temporal, block, frames)
        rows = slice(block * CHUNK, (block + 1) * CHUNK)
        row_id = lax.broadcasted_iota(jnp.int32, (CHUNK, 1), 0)
        for pair in range(PAIRS):
            cols = slice(pair * 128, pair * 128 + 128)
            q_a, q_b = split_heads(proj_ref[rows, cols], SCALE)
            keys = proj_ref[rows, D + pair * 128 : D + pair * 128 + 128]
            v_a, v_b = split_heads(proj_ref[rows, 2 * D + pair * 128 : 2 * D + pair * 128 + 128])
            scores = mm_nt(jnp.concatenate([q_a, q_b], axis=0), keys)
            scores = jnp.where(allowed, scores, NEGATIVE)
            top = jnp.max(scores, axis=1, keepdims=True)
            expo = jnp.exp(scores - top)
            total = jnp.sum(expo, axis=1, keepdims=True)
            soft = (expo / total).astype(BF)
            soft_ref[block * PAIRS + pair] = soft
            ctx_ref[rows, cols] = (mm(soft[:CHUNK], v_a) + mm(soft[CHUNK:], v_b)).astype(BF)
            for side in range(2):
                seen = jnp.where(row_id < valid[block], top[side * CHUNK : (side + 1) * CHUNK], NEGATIVE)
                best = jnp.max(seen, axis=0, keepdims=True)
                peaks = jnp.where(lane == 2 * pair + side, jnp.maximum(peaks, best), peaks)
    peak_ref[...] = peaks


def attend_backward(proj_ref, soft_ref, gctx_ref, gproj_ref):
    for block in range(BLOCKS):
        rows = slice(block * CHUNK, (block + 1) * CHUNK)
        for pair in range(PAIRS):
            cols = slice(pair * 128, pair * 128 + 128)
            kcols = slice(D + pair * 128, D + pair * 128 + 128)
            vcols = slice(2 * D + pair * 128, 2 * D + pair * 128 + 128)
            q_pair = jnp.concatenate(split_heads(proj_ref[rows, cols], SCALE), axis=0)
            k_a, k_b = split_heads(proj_ref[rows, kcols], SCALE)
            values = proj_ref[rows, vcols]
            g_pair = jnp.concatenate(split_heads(gctx_ref[rows, cols]), axis=0)
            soft_low = soft_ref[block * PAIRS + pair]
            soft = soft_low.astype(F32)
            grad_soft = mm_nt(g_pair, values)
            inner = jnp.sum(soft * grad_soft, axis=1, keepdims=True)
            grad_scores = (soft * (grad_soft - inner)).astype(BF)
            gproj_ref[rows, cols] = (mm(grad_scores[:CHUNK], k_a) + mm(grad_scores[CHUNK:], k_b)).astype(BF)
            gproj_ref[rows, kcols] = mm_tn(grad_scores, q_pair).astype(BF)
            gproj_ref[rows, vcols] = mm_tn(soft_low, g_pair).astype(BF)


def project(na_ref, qkv_ref, qv_ref, proj_ref):
    for part in range(3):
        cols = slice(part * D, (part + 1) * D)
        value = mm(na_ref[...], qkv_ref[:, cols])
        if part != 1:
            at = 0 if part == 0 else D
            value = value + qv_ref[:, at : at + D]
        proj_ref[:, cols] = value.astype(BF)


def space_forward_kernel(
    tok_ref, gain_ref, shift_ref, qkv_ref, qv_ref, out_ref, outb_ref,
    x1_ref, na_ref, proj_ref, soft_ref, ctx_ref, peak_ref, rows_ref,
):
    count = tok_ref.shape[0]
    flat = tok_ref[...].astype(F32)
    rows_ref[0:count, :] = flat
    rows_ref[CHUNK : CHUNK + PATCHES, :] = flat[PATCHES:, :]
    rows_ref[PATCHES:CHUNK, :] = jnp.zeros((CHUNK - PATCHES, D), F32)
    rows_ref[CHUNK + PATCHES :, :] = jnp.zeros((CHUNK - PATCHES, D), F32)
    unit, _ = row_stats(rows_ref[...])
    na_ref[...] = (unit * gain_ref[...] + shift_ref[...]).astype(BF)
    project(na_ref, qkv_ref, qv_ref, proj_ref)
    attend_forward(proj_ref, ctx_ref, soft_ref, peak_ref, False, 0, (PATCHES, PATCHES))
    rows_ref[...] = rows_ref[...] + mm(ctx_ref[...], out_ref[...]) + outb_ref[...]
    shares, frames, width = x1_ref.shape[0], x1_ref.shape[1], x1_ref.shape[2]
    for share in range(shares):
        for frame in range(frames):
            start = frame * CHUNK + share * width
            x1_ref[share, frame] = rows_ref[start : start + width, :].astype(BF)


def interleave(parts_ref, stripes_ref, rows_ref):
    shares, frames, width = parts_ref.shape[0], parts_ref.shape[1], parts_ref.shape[2]
    total = shares * frames
    for stripe in range(D // 128):
        cols = slice(stripe * 128, stripe * 128 + 128)
        for share in range(shares):
            for frame in range(frames):
                stripes_ref[stripe, pl.ds(share * frames + frame, width, stride=total), :] = parts_ref[
                    share, frame, :, cols
                ].astype(F32)
        stripes_ref[stripe, total * width :, :] = jnp.zeros((ROWS - total * width, 128), F32)
        rows_ref[:, cols] = stripes_ref[stripe].astype(rows_ref.dtype)


def separate(rows, stripes_ref, parts_ref):
    shares, frames, width = parts_ref.shape[0], parts_ref.shape[1], parts_ref.shape[2]
    total = shares * frames
    for stripe in range(D // 128):
        cols = slice(stripe * 128, stripe * 128 + 128)
        stripes_ref[stripe] = rows[:, cols]
        for share in range(shares):
            for frame in range(frames):
                parts_ref[share, frame, :, cols] = stripes_ref[
                    stripe, pl.ds(share * frames + frame, width, stride=total), :
                ].astype(parts_ref.dtype)


def time_forward_kernel(
    parts_ref, gain_ref, shift_ref, qkv_ref, qv_ref, out_ref, outb_ref,
    x1_ref, x2_ref, na_ref, proj_ref, soft_ref, ctx_ref, peak_ref, stripes_ref,
):
    frames = parts_ref.shape[0] * parts_ref.shape[1]
    count = frames * parts_ref.shape[2]
    interleave(parts_ref, stripes_ref, x1_ref)
    unit, _ = row_stats(x1_ref[...])
    na_ref[...] = (unit * gain_ref[...] + shift_ref[...]).astype(BF)
    project(na_ref, qkv_ref, qv_ref, proj_ref)
    attend_forward(proj_ref, ctx_ref, soft_ref, peak_ref, True, frames, (CHUNK, count - CHUNK))
    x2_ref[...] = x1_ref[...] + mm(ctx_ref[...], out_ref[...]) + outb_ref[...]


def mlp_kernel(
    x2_ref, gy_ref, gain_ref, shift_ref, in_ref, inb_ref, out_ref, outb_ref,
    mixed_ref, g2_ref, gin_ref, gout_ref, ggain_ref, gshift_ref, ginb_ref, goutb_ref,
    n2_ref, gyl_ref, rows_ref, back_ref, stripes_ref,
):
    step = pl.program_id(0)

    @pl.when(step == 0)
    def _():
        unit, _ = row_stats(x2_ref[...])
        n2_ref[...] = (unit * gain_ref[...] + shift_ref[...]).astype(BF)
        interleave(gy_ref, stripes_ref, gyl_ref)
        goutb_ref[...] = column_sum(gyl_ref[...])
        rows_ref[...] = jnp.zeros_like(rows_ref)
        back_ref[...] = jnp.zeros_like(back_ref)

    hidden = mm(n2_ref[...], in_ref[...]) + inb_ref[...]
    cumulative = 0.5 * (1.0 + lax.erf(hidden * (2.0 ** -0.5)))
    act = (hidden * cumulative).astype(BF)
    slope = cumulative + hidden * jnp.exp(-0.5 * hidden * hidden) * 0.3989422804014327
    rows_ref[...] += mm(act, out_ref[...])
    gout_ref[...] = mm_tn(act, gyl_ref[...]).astype(BF)
    ghid = (mm_nt(gyl_ref[...], out_ref[...]) * slope).astype(BF)
    ginb_ref[...] = column_sum(ghid)
    gin_ref[...] = mm_tn(n2_ref[...], ghid).astype(BF)
    back_ref[...] += mm_nt(ghid, in_ref[...])

    @pl.when(step == pl.num_programs(0) - 1)
    def _():
        separate(x2_ref[...] + rows_ref[...] + outb_ref[...], stripes_ref, mixed_ref)
        unit, inverse = row_stats(x2_ref[...])
        grad = back_ref[...]
        ggain_ref[...] = column_sum(grad * unit)
        gshift_ref[...] = column_sum(grad)
        g2_ref[...] = gyl_ref[...].astype(F32) + norm_backward(grad, unit, inverse, gain_ref[...])


def branch_backward(g_ref, ctx_ref, proj_ref, soft_ref, out_ref, gout_ref, goutb_ref, gproj_ref, gqv_ref, gbr_ref, gctx_ref):
    gbr_ref[...] = g_ref[...].astype(BF)
    goutb_ref[...] = column_sum(gbr_ref[...])
    gctx_ref[...] = mm_nt(gbr_ref[...], out_ref[...]).astype(BF)
    gout_ref[...] = mm_tn(ctx_ref[...], gbr_ref[...]).astype(BF)
    attend_backward(proj_ref, soft_ref, gctx_ref, gproj_ref)
    gqv_ref[:, 0:D] = column_sum(gproj_ref[:, 0:D])
    gqv_ref[:, D:] = column_sum(gproj_ref[:, 2 * D :])


def projection_backward(gproj_ref, qkv_ref):
    total = mm_nt(gproj_ref[:, 0:D], qkv_ref[:, 0:D])
    for part in range(1, 3):
        cols = slice(part * D, (part + 1) * D)
        total = total + mm_nt(gproj_ref[:, cols], qkv_ref[:, cols])
    return total


def time_backward_kernel(
    g_ref, x1_ref, gain_ref, ctx_ref, proj_ref, soft_ref, qkv_ref, out_ref,
    parts_ref, gproj_ref, gout_ref, goutb_ref, gqv_ref, ggain_ref, gshift_ref,
    gbr_ref, gctx_ref, stripes_ref,
):
    branch_backward(g_ref, ctx_ref, proj_ref, soft_ref, out_ref, gout_ref, goutb_ref, gproj_ref, gqv_ref, gbr_ref, gctx_ref)
    grad = projection_backward(gproj_ref, qkv_ref)
    unit, inverse = row_stats(x1_ref[...])
    ggain_ref[...] = column_sum(grad * unit)
    gshift_ref[...] = column_sum(grad)
    separate(g_ref[...] + norm_backward(grad, unit, inverse, gain_ref[...]), stripes_ref, parts_ref)


def weight_grad_kernel(na_ref, gproj_ref, gqkv_ref):
    for part in range(3):
        cols = slice(part * D, (part + 1) * D)
        gqkv_ref[:, cols] = mm_tn(na_ref[...], gproj_ref[:, cols]).astype(BF)


def space_backward_kernel(
    parts_ref, na_ref, ctx_ref, proj_ref, soft_ref, out_ref,
    g_ref, gproj_ref, gout_ref, goutb_ref, gqv_ref, gqkv_ref,
    gbr_ref, gctx_ref,
):
    shares, frames, width = parts_ref.shape[0], parts_ref.shape[1], parts_ref.shape[2]
    for frame in range(frames):
        for share in range(shares):
            start = frame * CHUNK + share * width
            g_ref[start : start + width, :] = parts_ref[share, frame].astype(F32)
        g_ref[frame * CHUNK + PATCHES : (frame + 1) * CHUNK, :] = jnp.zeros((CHUNK - PATCHES, D), F32)
    branch_backward(g_ref, ctx_ref, proj_ref, soft_ref, out_ref, gout_ref, goutb_ref, gproj_ref, gqv_ref, gbr_ref, gctx_ref)
    weight_grad_kernel(na_ref, gproj_ref, gqkv_ref)


def space_input_kernel(tok_ref, g_ref, gain_ref, gproj_ref, qkv_ref, gtok_ref, ggain_ref, gshift_ref, rows_ref):
    count = tok_ref.shape[0]
    flat = tok_ref[...].astype(F32)
    rows_ref[0:count, :] = flat
    rows_ref[CHUNK : CHUNK + PATCHES, :] = flat[PATCHES:, :]
    rows_ref[PATCHES:CHUNK, :] = jnp.zeros((CHUNK - PATCHES, D), F32)
    rows_ref[CHUNK + PATCHES :, :] = jnp.zeros((CHUNK - PATCHES, D), F32)
    unit, inverse = row_stats(rows_ref[...])
    grad = projection_backward(gproj_ref, qkv_ref)
    ggain_ref[...] = column_sum(grad * unit)
    gshift_ref[...] = column_sum(grad)
    rows_ref[...] = g_ref[...] + norm_backward(grad, unit, inverse, gain_ref[...])
    gtok_ref[0:PATCHES, :] = rows_ref[0:PATCHES, :]
    gtok_ref[PATCHES:, :] = rows_ref[CHUNK : CHUNK + PATCHES, :]


def call(kernel, outs, scratch, flops, *operands, name):
    return pl.pallas_call(
        kernel,
        out_shape=[jax.ShapeDtypeStruct(shape, dtype) for shape, dtype in outs],
        scratch_shapes=[pltpu.VMEM(shape, dtype) for shape, dtype in scratch],
        compiler_params=pltpu.CompilerParams(vmem_limit_bytes=VMEM_LIMIT),
        cost_estimate=pl.CostEstimate(flops=flops, bytes_accessed=8 * 2**20, transcendentals=0),
        name=name,
    )(*operands)


def exchange(parts):
    return lax.all_to_all(parts, "seq", split_axis=0, concat_axis=0, tiled=True)


def on_device(
    tokens, norm_gain, norm_bias, attn_qkv, attn_qv_bias, attn_out, attn_out_bias,
    mlp_in, mlp_in_bias, mlp_out, mlp_out_bias, threshold, cotangent,
):
    clip_count, local_len, _ = tokens.shape
    seq = lax.axis_size("seq")
    frames = local_len // PATCHES
    width = PATCHES // seq
    ff = mlp_in.shape[1]
    split_shape = (seq, frames, width, D)
    tok = tokens.reshape(local_len, D)
    cot = jnp.swapaxes(cotangent.reshape(frames, seq, width, D), 0, 1)

    def gather(value, axis):
        return lax.all_gather(value, "fsdp", axis=axis, tiled=True)

    gain = gather(norm_gain, 1).astype(F32)
    shift = gather(norm_bias, 1).astype(F32)
    qv = gather(attn_qv_bias, 1).astype(F32)
    outb = gather(attn_out_bias, 1).astype(F32)
    inb = gather(mlp_in_bias, 0).astype(F32).reshape(1, ff)
    moutb = gather(mlp_out_bias, 0).astype(F32).reshape(1, D)
    qkv = [gather(attn_qkv[a], 0) for a in range(2)]
    out = [gather(attn_out[a], 0) for a in range(2)]
    w_in = gather(mlp_in, 0)
    w_out = gather(mlp_out, 0)

    def row(matrix, index):
        return matrix[index : index + 1]

    state = lambda: [
        ((ROWS, D), BF), ((ROWS, 3 * D), BF), ((BLOCKS * PAIRS, 2 * CHUNK, CHUNK), BF), ((ROWS, D), BF), ((8, 128), F32),
    ]
    attn_flops = 2 * ROWS * D * 4 * D + 4 * BLOCKS * H * CHUNK * CHUNK * HD
    parts, na0, proj0, soft0, ctx0, peak0 = call(
        space_forward_kernel, [(split_shape, BF)] + state(), [((ROWS, D), F32)], attn_flops,
        tok, row(gain, 0), row(shift, 0), qkv[0], row(qv, 0), out[0], row(outb, 0), name="space_forward",
    )
    parts = exchange(parts)
    x1, x2, na1, proj1, soft1, ctx1, peak1 = call(
        time_forward_kernel, [((ROWS, D), F32), ((ROWS, D), F32)] + state(), [((D // 128, ROWS, 128), F32)], attn_flops,
        parts, row(gain, 1), row(shift, 1), qkv[1], row(qv, 1), out[1], row(outb, 1), name="time_forward",
    )
    gy = exchange(cot)
    fixed = lambda *shape: pl.BlockSpec(shape, lambda i: (0,) * len(shape))
    mixed, g2, g_in, g_mout, ggain2, gshift2, g_inb, g_moutb = pl.pallas_call(
        mlp_kernel,
        grid=(ff // FF_BLOCK,),
        in_specs=[
            fixed(ROWS, D), fixed(*split_shape), fixed(1, D), fixed(1, D),
            pl.BlockSpec((D, FF_BLOCK), lambda i: (0, i)), pl.BlockSpec((1, FF_BLOCK), lambda i: (0, i)),
            pl.BlockSpec((FF_BLOCK, D), lambda i: (i, 0)), fixed(1, D),
        ],
        out_specs=[
            fixed(*split_shape), fixed(ROWS, D),
            pl.BlockSpec((D, FF_BLOCK), lambda i: (0, i)), pl.BlockSpec((FF_BLOCK, D), lambda i: (i, 0)),
            fixed(1, D), fixed(1, D), pl.BlockSpec((1, FF_BLOCK), lambda i: (0, i)), fixed(1, D),
        ],
        out_shape=[
            jax.ShapeDtypeStruct(split_shape, BF), jax.ShapeDtypeStruct((ROWS, D), F32),
            jax.ShapeDtypeStruct((D, ff), BF), jax.ShapeDtypeStruct((ff, D), BF),
            jax.ShapeDtypeStruct((1, D), F32), jax.ShapeDtypeStruct((1, D), F32),
            jax.ShapeDtypeStruct((1, ff), F32), jax.ShapeDtypeStruct((1, D), F32),
        ],
        scratch_shapes=[
            pltpu.VMEM((ROWS, D), BF), pltpu.VMEM((ROWS, D), BF), pltpu.VMEM((ROWS, D), F32), pltpu.VMEM((ROWS, D), F32),
            pltpu.VMEM((D // 128, ROWS, 128), F32),
        ],
        compiler_params=pltpu.CompilerParams(vmem_limit_bytes=VMEM_LIMIT),
        cost_estimate=pl.CostEstimate(flops=10 * ROWS * D * ff, bytes_accessed=20 * 2**20, transcendentals=0),
        name="mlp",
    )(x2, gy, row(gain, 2), row(shift, 2), w_in, inb, w_out, moutb)
    mixed = exchange(mixed)
    small = [((1, D), F32), ((1, 2 * D), F32)]
    gparts, gproj1, g_out1, g_outb1, g_qv1, ggain1, gshift1 = call(
        time_backward_kernel,
        [(split_shape, BF), ((ROWS, 3 * D), BF), ((D, D), BF)] + small + [((1, D), F32)] * 2,
        [((ROWS, D), BF), ((ROWS, D), BF), ((D // 128, ROWS, 128), F32)], 2 * attn_flops,
        g2, x1, row(gain, 1), ctx1, proj1, soft1, qkv[1], out[1], name="time_backward",
    )
    gparts = exchange(gparts)
    (g_qkv1,) = call(weight_grad_kernel, [((D, 3 * D), BF)], [], attn_flops, na1, gproj1, name="time_weight_grad")
    g1, gproj0, g_out0, g_outb0, g_qv0, g_qkv0 = call(
        space_backward_kernel,
        [((ROWS, D), F32), ((ROWS, 3 * D), BF), ((D, D), BF)] + small + [((D, 3 * D), BF)],
        [((ROWS, D), BF), ((ROWS, D), BF)], 2 * attn_flops,
        gparts, na0, ctx0, proj0, soft0, out[0], name="space_backward",
    )
    g_tok, ggain0, gshift0 = call(
        space_input_kernel, [((local_len, D), F32), ((1, D), F32), ((1, D), F32)], [((ROWS, D), F32)], attn_flops,
        tok, g1, row(gain, 0), gproj0, qkv[0], name="space_input",
    )

    def scatter(value, axis):
        return lax.psum_scatter(value, "fsdp", scatter_dimension=axis, tiled=True)

    def total(value, axis):
        return lax.psum(scatter(value, axis).astype(BF), "seq").astype(F32)

    grad_qkv = jnp.stack([total(g_qkv0, 0), total(g_qkv1, 0)])
    grad_out = jnp.stack([total(g_out0, 0), total(g_out1, 0)])
    grad_in = total(g_in, 0)
    grad_mout = total(g_mout, 0)
    grad_gain = lax.psum(scatter(jnp.concatenate([ggain0, ggain1, ggain2]), 1), "seq")
    grad_shift = lax.psum(scatter(jnp.concatenate([gshift0, gshift1, gshift2]), 1), "seq")
    grad_qv = lax.psum(scatter(jnp.concatenate([g_qv0, g_qv1]), 1), "seq")
    grad_outb = lax.psum(scatter(jnp.concatenate([g_outb0, g_outb1]), 1), "seq")
    grad_inb = lax.psum(scatter(g_inb[0], 0), "seq")
    grad_moutb = lax.psum(scatter(g_moutb[0], 0), "seq")

    peak_pair = jnp.stack([peak0[0, :H], peak1[0, :H]])
    logit_max = lax.pmax(peak_pair, ("fsdp", "seq"))
    factor = threshold / jnp.maximum(logit_max, threshold)
    column_scale = jnp.repeat(jnp.sqrt(factor), HD, axis=1)
    clipped = attn_qkv[:, :, : 2 * D].astype(F32) * jnp.concatenate([column_scale, column_scale], axis=1)[:, None, :]
    mixed = jnp.swapaxes(mixed, 0, 1).reshape(tokens.shape)
    return (
        mixed, g_tok.reshape(tokens.shape), grad_gain, grad_shift, grad_qkv, grad_qv, grad_out, grad_outb,
        grad_in, grad_inb, grad_mout, grad_moutb, logit_max, clipped,
    )


def solution(mesh):
    placed = (
        P("fsdp", "seq", None), P(None, "fsdp"), P(None, "fsdp"), P(None, "fsdp", None), P(None, "fsdp"),
        P(None, "fsdp", None), P(None, "fsdp"), P("fsdp", None), P("fsdp"), P("fsdp", None), P("fsdp"), P(),
        P("fsdp", "seq", None),
    )
    return jax.shard_map(
        on_device,
        mesh=mesh,
        in_specs=placed,
        out_specs=(
            P("fsdp", "seq", None), P("fsdp", "seq", None), P(None, "fsdp"), P(None, "fsdp"), P(None, "fsdp", None),
            P(None, "fsdp"), P(None, "fsdp", None), P(None, "fsdp"), P("fsdp", None), P("fsdp"), P("fsdp", None),
            P("fsdp"), P(), P(None, "fsdp", None),
        ),
        check_vma=False,
    )
```

time: 1200 us -> 821 us (0.68)
  local copies, waits for them, and re-layouts: 202 us -> 27.7 us
  matrix products: 119 us -> 0 us
  waiting for transfers between devices: 597 us -> 510 us
  other arithmetic: 95.1 us -> 8.77 us
  Pallas kernels: 0 us -> 81.6 us
  blocking collectives: 132 us -> 153 us
  starting transfers between devices: 32.2 us -> 15.5 us
    all_to_all x8 -> x3, waiting for transfers between devices: 315 us -> 0.01 us  [exchange(): return lax.all_to_all(parts, 'seq', split_axis=0, concat_axis=0, tiled=True)]
    reduce_scatter x4 -> x6, waiting for transfers between devices: 118 us -> 238 us  [scatter(): return lax.psum_scatter(value, 'fsdp', scatter_dimension=axis, tiled=True)]
    dot_general x30 -> x0, matrix products: 119 us -> none  [the longest x6 34 us: rows_inner(): lax.dot_general(left_side, right_side, (((0,), (0,)), ((), ())), preferre...]
    all_gather x4 -> x6, waiting for transfers between devices: 23.1 us -> 107 us  [gather(): return lax.all_gather(value, 'fsdp', axis=axis, tiled=True)]
    pallas_call x0 -> x7, Pallas kernels: none -> 81.6 us  [the longest x6 59.8 us: call(): pl.pallas_call(kernel, out_shape=[jax.ShapeDtypeStruct(shape, dtype) for...]
    all_to_all x18 -> x3, local copies, waits for them, and re-layouts: 61.2 us -> 2.75 us  [exchange(): return lax.all_to_all(parts, 'seq', split_axis=0, concat_axis=0, tiled=True)]
    reshape x20 -> x4, local copies, waits for them, and re-layouts: 52.3 us -> 1.89 us  [the longest x1 1.02 us: on_device(): mixed = jnp.swapaxes(mixed, 0, 1).reshape(tokens.shape)]
    another operation x27 -> x0, local copies, waits for them, and re-layouts: 35.6 us -> none  [the longest x8 18.9 us: attention_backward(): jnp.stack([restore(grad_queries, temporal, clip_count), restore(grad_keys...]
  transfers between devices with their start and end apart: 21 -> 20, of which waited for: 14 -> 13; matrix products, arithmetic and copies ran while one was open for 25% -> 4% of each run, Pallas kernels for 0% -> 5%
where the time goes in v1:
time: 821 us; the launch traced here: 814 us
  waiting for transfers between devices  510 us (62%)
  blocking collectives  153 us (19%)
  Pallas kernels  81.6 us (10%)
  local copies, waits for them, and re-layouts  27.7 us (3%)
  between operations  16.8 us (2%)
  starting transfers between devices  15.5 us (2%)
  other arithmetic  8.77 us (1%)
    reduce_scatter x6, waiting for transfers between devices, scatter(): return lax.psum_scatter(value, 'fsdp', scatter_dimension=axis, tiled=True)  238 us
    all_gather x6, waiting for transfers between devices, gather(): return lax.all_gather(value, 'fsdp', axis=axis, tiled=True)  107 us
    psum x1, waiting for transfers between devices, total(): return lax.psum(scatter(value, axis).astype(BF), 'seq').astype(F32)  86.5 us
    unnamed x21, waiting for transfers between devices  78.9 us
    pallas_call x6, Pallas kernels, call(): pl.pallas_call(kernel, out_shape=[jax.ShapeDtypeStruct(shape, dtype) for...  59.8 us
    all_gather x5, blocking collectives, gather(): return lax.all_gather(value, 'fsdp', axis=axis, tiled=True)  43.3 us
    pmax x1, blocking collectives, on_device(): logit_max = lax.pmax(peak_pair, ('fsdp', 'seq'))  39.4 us
    unnamed x2, blocking collectives  36.5 us
  transfers between devices with their start and end apart: 20, of which 13 were waited for; matrix products, arithmetic and copies ran while one was open for 4% of the time, Pallas kernels for 5%

profile of v1, /device:TPU:0, one launch (start us, length us, event | category | flops | bytes accessed | tf_op | source)
XLA Modules:
  0.0 814.0 jit_solution(17433178562614023963)
XLA Ops:
  30.5 8.9 %all-gather.4 = bf16[8,96,3]{1,2,0:T(4,128)(2,1)S(1)} all-gather(bf16[1,96,3]{1,2,0:T(4,128)(2,1)S(1)} %bitcast.69), channel_id=1, replica_groups=mesh['fsdp'=8,'seq'=4] {'fsdp'}, dimensions={0}, use_global_device_ids=true | all-gather | bytes 5184 | tf_op jit(solution)/shard_map/all_gather | solution.py:336
  58.3 15.5 %all-gather.20.cloned.1.call-done = bf16[1,768,2304]{2,1,0:T(8,128)(2,1)} async-done(((bf16[1,96,2304]{2,1,0:T(8,128)(2,1)}), bf16[1,768,2304]{2,1,0:T(8,128)(2,1)}) %all-gather.20.cloned.1.call-update) | async-done | bytes 3538960 | tf_op jit(solution)/shard_map/all_gather | solution.py:336
  73.8 9.1 %space_forward.1 = (bf16[4,2,49,768]{3,2,1,0:T(8,128)(2,1)}, bf16[416,768]{1,0:T(8,128)(2,1)}, bf16[416,2304]{1,0:T(8,128)(2,1)}, bf16[12,416,208]{2,1,0:T(8,128...) custom-call(bf16[392,768]{1,0:T(8,128)(2,1)} %bitcast.81, f32[1,768]{1,0:T(1,128)} %get-tuple-element.118.gain_ref, ...), custom_call_target="tpu_custom_call" | custom-call | flops 2228748288 | bytes 8388608 | tf_op jit(solution)/shard_map/space_forward/pallas_call | solution.py:308
  91.4 13.5 %all-reduce = bf16[768]{0:T(1024)(128)(2,1)S(1)} all-reduce(bf16[768]{0:T(1024)(128)(2,1)S(1)} %dynamic-update-slice), channel_id=1, replica_groups=mesh['fsdp'=8,'seq'=4] {'fsdp'}, use_global_device_ids=true, to_apply=%add | all-reduce | flops 768 | bytes 3072
  105.5 9.0 %all-gather.8 = bf16[8,1,384]{2,1,0:T(2,128)(2,1)S(1)} all-gather(bf16[1,1,384]{2,1,0:T(2,128)(2,1)S(1)} %reshape.82), channel_id=1, replica_groups=mesh['fsdp'=8,'seq'=4] {'fsdp'}, dimensions={0}, use_global_device_ids=true | all-gather | bytes 6912 | tf_op jit(solution)/shard_map/all_gather | solution.py:336
  116.9 19.8 %all-gather.24.cloned.1.call-done = bf16[1,768,2304]{2,1,0:T(8,128)(2,1)} async-done(((bf16[1,96,2304]{2,1,0:T(8,128)(2,1)}), bf16[1,768,2304]{2,1,0:T(8,128)(2,1)}) %all-gather.24.cloned.1.call-update) | async-done | bytes 3538960 | tf_op jit(solution)/shard_map/all_gather | solution.py:336
  136.8 9.9 %time_forward.1 = (f32[416,768]{1,0:T(8,128)}, f32[416,768]{1,0:T(8,128)}, bf16[416,768]{1,0:T(8,128)(2,1)}, bf16[416,2304]{1,0:T(8,128)(2,1)}, bf16[12,416,208]...) custom-call(bf16[4,2,49,768]{3,2,1,0:T(8,128)(2,1)} %copy.54.parts_ref, ...), custom_call_target="tpu_custom_call" | custom-call | flops 2228748288 | bytes 8388608 | tf_op jit(solution)/shard_map/time_forward/pallas_call | solution.py:308
  146.6 30.8 %all-gather.16.cloned.1.call-done.in_ref = bf16[768,3072]{1,0:T(8,128)(2,1)} async-done(((bf16[96,3072]{1,0:T(8,128)(2,1)}), bf16[768,3072]{1,0:T(8,128)(2,1)}) %all-gather.16.cloned.1.call-update) | async-done | bytes 4718608 | tf_op jit(solution)/shard_map/all_gather | solution.py:336
  177.5 40.7 %all-gather.18.cloned.1.call-done.out_ref = bf16[3072,768]{1,0:T(8,128)(2,1)} async-done(((bf16[384,768]{1,0:T(8,128)(2,1)}), bf16[3072,768]{1,0:T(8,128)(2,1)}) %all-gather.18.cloned.1.call-update) | async-done | bytes 4718608 | tf_op jit(solution)/shard_map/all_gather | solution.py:336
  218.1 21.9 %mlp.1 = (bf16[4,2,49,768]{3,2,1,0:T(8,128)(2,1)}, f32[416,768]{1,0:T(8,128)}, bf16[768,3072]{1,0:T(8,128)(2,1)}, bf16[3072,768]{1,0:T(8,128)(2,1)}, f32[1,768]{...) custom-call(f32[416,768]{1,0:T(8,128)} %get-tuple-element.52.x2_ref, ...), custom_call_target="tpu_custom_call" | custom-call | flops 9814671360 | bytes 20971520 | tf_op jit(solution)/shard_map/mlp/pallas_call | solution.py:367
  240.0 15.0 %time_backward.1 = (bf16[4,2,49,768]{3,2,1,0:T(8,128)(2,1)}, bf16[416,2304]{1,0:T(8,128)(2,1)}, bf16[768,768]{1,0:T(8,128)(2,1)}, f32[1,768]{1,0:T(1,128)}, f32[...) custom-call(f32[416,768]{1,0:T(8,128)} %get-tuple-element.54.g_ref, f32[416,768]{1,0:T(8,128)} %get-tuple-element.55.x1_ref, ...), custom_call_target="tpu_custom_call" | custom-call | flops 4457496576 | bytes 8388608 | tf_op jit(solution)/shard_map/time_backward/pallas_call | solution.py:308
  256.7 21.2 %all_to_all.20 = bf16[4,2,49,768]{3,1,2,0:T(2,128)(2,1)S(1)} all-to-all(bf16[4,2,49,768]{3,1,2,0:T(2,128)(2,1)S(1)} %copy.59), channel_id=1, replica_groups=mesh['fsdp'=8,'seq'=4] {'seq'}, dimensions={0} | all-to-all | bytes 1204224 | tf_op jit(solution)/shard_map/all_to_all | solution.py:319
  278.9 13.7 %space_backward.1 = (f32[416,768]{1,0:T(8,128)}, bf16[416,2304]{1,0:T(8,128)(2,1)}, bf16[768,768]{1,0:T(8,128)(2,1)}, f32[1,768]{1,0:T(1,128)}, f32[1,1536]{1,0:T(1,128)}, /*index=5*/bf16[768,2304]{1,0:T(8,128)(2,1)}) custom-call(bf16[4,2,49,768]{3,2,1,0:T(8,128)(2,1)} %copy.60.parts_ref, bf16[416,768]{1,0:T(8,128)(2,1)} %get-tuple-element.60.na_ref, ...), custom_call_target="tpu_custom_call" | custom-call | flops 4457496576 | bytes 8388608 | tf_op jit(solution)/shard_map/space_backward/pallas_call | solution.py:308
  312.9 20.0 %reduce-scatter.23.cloned.1.call-done = bf16[96,768]{1,0:T(8,128)(2,1)} async-done(((bf16[768,768]{1,0:T(8,128)(2,1)}), bf16[96,768]{1,0:T(8,128)(2,1)}) %reduce-scatter.23.cloned.1.call-update) | async-done | bytes 147472 | tf_op jit(solution)/shard_map/reduce_scatter | solution.py:416
  333.0 51.6 %reduce-scatter.21.cloned.1.call-done = bf16[96,2304]{1,0:T(8,128)(2,1)} async-done(((bf16[768,2304]{1,0:T(8,128)(2,1)}), bf16[96,2304]{1,0:T(8,128)(2,1)}) %reduce-scatter.21.cloned.1.call-update) | async-done | bytes 442384 | tf_op jit(solution)/shard_map/reduce_scatter | solution.py:416
  384.6 51.4 %reduce-scatter.19.cloned.1.call-done = bf16[96,2304]{1,0:T(8,128)(2,1)} async-done(((bf16[768,2304]{1,0:T(8,128)(2,1)}), bf16[96,2304]{1,0:T(8,128)(2,1)}) %reduce-scatter.19.cloned.1.call-update) | async-done | bytes 442384 | tf_op jit(solution)/shard_map/reduce_scatter | solution.py:416
  436.1 57.3 %reduce-scatter.27.cloned.1.call-done = bf16[96,3072]{1,0:T(8,128)(2,1)} async-done(((bf16[768,3072]{1,0:T(8,128)(2,1)}), bf16[96,3072]{1,0:T(8,128)(2,1)}) %reduce-scatter.27.cloned.1.call-update) | async-done | bytes 589840 | tf_op jit(solution)/shard_map/reduce_scatter | solution.py:416
  493.4 57.6 %reduce-scatter.29.cloned.1.call-done = bf16[384,768]{1,0:T(8,128)(2,1)} async-done(((bf16[3072,768]{1,0:T(8,128)(2,1)}), bf16[384,768]{1,0:T(8,128)(2,1)}) %reduce-scatter.29.cloned.1.call-update) | async-done | bytes 589840 | tf_op jit(solution)/shard_map/reduce_scatter | solution.py:416
  553.8 39.4 %pmax.7 = f32[2,12]{1,0:T(2,128)S(1)} all-reduce(f32[2,12]{1,0:T(2,128)S(1)} %pad_maximum_fusion.5), channel_id=1, replica_groups=mesh['fsdp'=8,'seq'=4] {'fsdp','seq'}, use_global_device_ids=true, to_apply=%region_24.0 | all-reduce | flops 24 | bytes 192 | tf_op jit(solution)/shard_map/pmax | solution.py:433
  599.5 23.0 %all-reduce.3 = (f32[3072]{0:T(1024)S(1)}, f32[768]{0:T(1024)S(1)}) all-reduce(f32[3072]{0:T(1024)S(1)} %bitcast.68, f32[768]{0:T(1024)S(1)} %reduce), channel_id=15, replica_groups=mesh['fsdp'=8,'seq'=4] {'fsdp'}, use_global_device_ids=true, to_apply=%region_18.0.clone | all-reduce | flops 3840 | bytes 30720
  626.1 36.5 %reduce-scatter.31.cloned.1.call-done = f32[96,3]{1,0:T(8,128)} async-done(((f32[768,3]{1,0:T(8,128)}), f32[96,3]{1,0:T(8,128)}) %reduce-scatter.31.cloned.1.call-update) | async-done | bytes 1168
  663.5 37.7 %reduce-scatter.35.cloned.1.call-done = f32[192,2]{1,0:T(8,128)} async-done(((f32[1536,2]{1,0:T(8,128)}), f32[192,2]{1,0:T(8,128)}) %reduce-scatter.35.cloned.1.call-update) | async-done | bytes 1552
  702.2 12.8 %all-reduce.4 = (f32[3,96]{1,0:T(4,128)}, f32[3,96]{1,0:T(4,128)}, f32[2,192]{1,0:T(2,128)}, f32[2,96]{1,0:T(2,128)}, f32[384]{0:T(512)}, /*index=5*/f32[96]{0:T(128)}) all-reduce(f32[3,96]{1,0:T(4,128)S(1)} %copy.62, f32[3,96]{1,0:T(4,128)S(1)} %copy.64, f32[2,192]{1,0:T(2,128)S(1)} %copy.66, ...), channel_id=1, replica_groups=mesh['fsdp'=8,'seq'=4] {'seq'}, use_global_device_ids=true, to_apply=%region_1.0 | all-reduce | flops 1632 | bytes 13056 | tf_op jit(solution)/shard_map/psum | solution.py:425
  714.9 86.5 %all-reduce.8.cloned.1.call-done = (bf16[1,96,2304]{2,1,0:T(8,128)(2,1)}, bf16[1,96,2304]{2,1,0:T(8,128)(2,1)}, bf16[1,96,768]{2,1,0:T(8,128)(2,1)}, bf16[1,96,7...) async-done(((bf16[1,96,2304]{2,1,0:T(8,128)(2,1)}, bf16[1,96,2304]{2,1,0:T(8,128)(2,1)}, bf16[1,96,768]{2,1,0:T(8,128)(2,1)}, ...) | async-done | bytes 2359312 | tf_op jit(solution)/shard_map/psum | solution.py:419
  (160 shorter events, 94.3 us)
Async XLA Ops:
  7.2 51.1 %all-gather.22.cloned.1.call-start = ((), (), s32[]{:S(2)}) async-start(), calls=%async_computation.23 | async-start | bytes 1327104 | tf_op jit(solution)/shard_map/all_gather | solution.py:336
  9.0 64.8 %all-gather.20.cloned.1.call-start = ((), (), s32[]{:S(2)}) async-start(), calls=%async_computation.22 | async-start | bytes 3981312 | tf_op jit(solution)/shard_map/all_gather | solution.py:336
  11.2 105.7 %all-gather.26.cloned.1.call-start = ((), (), s32[]{:S(2)}) async-start(), calls=%async_computation.25 | async-start | bytes 1327104 | tf_op jit(solution)/shard_map/all_gather | solution.py:336
  11.9 124.8 %all-gather.24.cloned.1.call-start = ((), (), s32[]{:S(2)}) async-start(), calls=%async_computation.24 | async-start | bytes 3981312 | tf_op jit(solution)/shard_map/all_gather | solution.py:336
  12.5 164.9 %all-gather.16.cloned.1.call-start = ((), (), s32[]{:S(2)}) async-start(), calls=%async_computation.14 | async-start | bytes 5308416 | tf_op jit(solution)/shard_map/all_gather | solution.py:336
  13.1 205.0 %all-gather.18.cloned.1.call-start = ((), (), s32[]{:S(2)}) async-start(), calls=%async_computation.15 | async-start | bytes 5308416 | tf_op jit(solution)/shard_map/all_gather | solution.py:336
  13.7 33.6 %copy-start.22 = (bf16[2,192]{1,0:T(2,128)(2,1)S(1)}, bf16[2,192]{1,0:T(2,128)(2,1)}, u32[]{:S(2)}) copy-start(bf16[2,192]{1,0:T(2,128)(2,1)} %param.17) | copy-start | bytes 2308
  15.4 69.9 %all-to-all-start.1 = ((bf16[4,2,49,768]{3,1,2,0:T(2,128)(2,1)}), bf16[4,2,49,768]{3,1,2,0:T(2,128)(2,1)S(1)}, u32[]{:S(2)}, u32[]{:S(2)}) async-start(bf16[4,2,49,768]{3,1,2,0:T(2,128)(2,1)} %copy.55), calls=%async_computation.1 | async-start | bytes 1204224 | tf_op jit(solution)/shard_map/all_to_all | solution.py:319
  85.3 30.7 %all-to-all-start = ((bf16[4,2,49,768]{3,1,2,0:T(2,128)(2,1)}), bf16[4,2,49,768]{3,1,2,0:T(2,128)(2,1)S(1)}, u32[]{:S(2)}, u32[]{:S(2)}) async-start(bf16[4,2,49,768]{3,1,2,0:T(2,128)(2,1)} %copy.53), calls=%async_computation | async-start | bytes 1204224 | tf_op jit(solution)/shard_map/all_to_all | solution.py:319
  89.9 223.0 %reduce-scatter.25.cloned.1.call-start = ((), (), s32[]{:S(2)}) async-start(), calls=%async_computation.19 | async-start | bytes 1327104 | tf_op jit(solution)/shard_map/reduce_scatter | solution.py:416
  255.1 77.9 %reduce-scatter.23.cloned.1.call-start = ((), (), s32[]{:S(2)}) async-start(), calls=%async_computation.18 | async-start | bytes 1327104 | tf_op jit(solution)/shard_map/reduce_scatter | solution.py:416
  292.6 92.0 %reduce-scatter.21.cloned.1.call-start = ((), (), s32[]{:S(2)}) async-start(), calls=%async_computation.17 | async-start | bytes 3981312 | tf_op jit(solution)/shard_map/reduce_scatter | solution.py:416
  298.2 137.9 %reduce-scatter.19.cloned.1.call-start = ((), (), s32[]{:S(2)}) async-start(), calls=%async_computation.16 | async-start | bytes 3981312 | tf_op jit(solution)/shard_map/reduce_scatter | solution.py:416
  298.8 194.6 %reduce-scatter.27.cloned.1.call-start = ((), (), s32[]{:S(2)}) async-start(), calls=%async_computation.20 | async-start | bytes 5308416 | tf_op jit(solution)/shard_map/reduce_scatter | solution.py:416
  299.5 251.5 %reduce-scatter.29.cloned.1.call-start = ((), (), s32[]{:S(2)}) async-start(), calls=%async_computation.21 | async-start | bytes 5308416 | tf_op jit(solution)/shard_map/reduce_scatter | solution.py:416
  300.1 323.7 %reduce-scatter.37.cloned.1.call-start = ((), (), s32[]{:S(2)}) async-start(), calls=%async_computation.29 | async-start | bytes 442368
  307.8 317.5 %reduce-scatter.33.cloned.1.call-start = ((), (), s32[]{:S(2)}) async-start(), calls=%async_computation.27 | async-start | bytes 442368
  309.5 353.1 %reduce-scatter.31.cloned.1.call-start = ((), (), s32[]{:S(2)}) async-start(), calls=%async_computation.26 | async-start | bytes 442368
  311.3 389.9 %reduce-scatter.35.cloned.1.call-start = ((), (), s32[]{:S(2)}) async-start(), calls=%async_computation.28 | async-start | bytes 884736
  312.8 280.3 %copy-start.1 = (bf16[4,2,49,768]{3,2,1,0:T(8,128)(2,1)S(1)}, bf16[4,2,49,768]{3,2,1,0:T(8,128)(2,1)}, u32[]{:S(2)}) copy-start(bf16[4,2,49,768]{3,2,1,0:T(8,128)(2,1)} %get-tuple-element.53) | copy-start | bytes 1806340
  312.9 488.6 %all-reduce.8.cloned.1.call-start = ((), (), s32[]{:S(2)}) async-start(), calls=%async_computation.30 | async-start | bytes 4718592 | tf_op jit(solution)/shard_map/psum | solution.py:419
  551.0 47.1 %copy-start.23 = (f32[2,12]{1,0:T(2,128)S(1)}, f32[2,12]{1,0:T(2,128)}, u32[]{:S(2)}) copy-start(f32[2,12]{1,0:T(2,128)} %param.24) | copy-start | bytes 292
  551.0 47.3 %copy-start = (bf16[2,96,2304]{2,1,0:T(8,128)(2,1)S(1)}, bf16[2,96,2304]{2,1,0:T(8,128)(2,1)}, u32[]{:S(2)}) copy-start(bf16[2,96,2304]{2,1,0:T(8,128)(2,1)} %param.16) | copy-start | bytes 2654212
  594.5 28.3 %all-to-all-start.2 = ((bf16[4,2,49,768]{3,1,2,0:T(2,128)(2,1)}), bf16[4,2,49,768]{3,1,2,0:T(2,128)(2,1)S(1)}, u32[]{:S(2)}, u32[]{:S(2)}) async-start(bf16[4,2,49,768]{3,1,2,0:T(2,128)(2,1)} %copy.57), calls=%async_computation.2 | async-start | bytes 1204224 | tf_op jit(solution)/shard_map/all_to_all | solution.py:319
  (23 other events, 146.1 us)
Sparse Core Ops, SparseCore 0:
  10.5 26.7 all-gather.21
  39.7 33.9 all-gather.19
  76.2 24.1 all-gather.25
  102.7 33.9 all-gather.23
  138.5 38.9 all-gather.15
  179.2 38.9 all-gather.17
  255.2 36.7 reduce-scatter.24
  296.2 36.7 reduce-scatter.22
  336.5 48.0 reduce-scatter.20
  387.9 48.0 reduce-scatter.18
  439.5 53.8 reduce-scatter.26
  497.1 53.8 reduce-scatter.28
  554.1 33.7 reduce-scatter.36
  591.4 33.8 reduce-scatter.32
  628.7 33.8 reduce-scatter.30
  666.2 34.9 reduce-scatter.34
  703.9 97.5 all-reduce.7

commit v2 on v1

v2 whole, which is shorter than its diff:
```python
import functools
import itertools

import jax
import jax.numpy as jnp
from jax import lax
from jax.experimental import pallas as pl
from jax.experimental.pallas import tpu as pltpu
from jax.sharding import PartitionSpec as P

H = 12
PATCHES = 196
HD = 64
D = 768
PAIRS = H // 2
CHUNK = 208
BLOCKS = 2
ROWS = BLOCKS * CHUNK
FF_BLOCK = 768
EPSILON = 1e-06
NEGATIVE = -1e30
SCALE = HD ** (-0.5)
COST = 1000
VMEM_LIMIT = 58 * 1024 * 1024
BF = jnp.bfloat16
F32 = jnp.float32


def mm(a, b):
    return lax.dot_general(a, b, (((1,), (0,)), ((), ())), preferred_element_type=F32)


def mm_nt(a, b):
    return lax.dot_general(a, b, (((1,), (1,)), ((), ())), preferred_element_type=F32)


def mm_tn(a, b):
    return lax.dot_general(a, b, (((0,), (0,)), ((), ())), preferred_element_type=F32)


def row_stats(rows):
    centre = jnp.mean(rows, axis=-1, keepdims=True)
    centred = rows - centre
    second = jnp.mean(centred * centred, axis=-1, keepdims=True)
    inverse = lax.rsqrt(second + EPSILON)
    return centred * inverse, inverse


def norm_backward(grad, unit, inverse, gain):
    weighted = grad * gain
    first = jnp.mean(weighted, axis=-1, keepdims=True)
    second = jnp.mean(weighted * unit, axis=-1, keepdims=True)
    return (weighted - first - unit * second) * inverse


def column_sum(values):
    return jnp.sum(values.astype(F32), axis=0, keepdims=True)


def masks(temporal, block, frames):
    row = lax.broadcasted_iota(jnp.int32, (2 * CHUNK, CHUNK), 0)
    col = lax.broadcasted_iota(jnp.int32, (2 * CHUNK, CHUNK), 1)
    if temporal:
        row = jnp.where(row >= CHUNK, row - CHUNK, row)
        allowed = (row // frames) == (col // frames)
    else:
        allowed = col < PATCHES
    return allowed


def lower_lanes(rows):
    return lax.broadcasted_iota(jnp.int32, (rows, 2 * HD), 1) < HD


def split_heads(pair, scale=None):
    low_half = lower_lanes(pair.shape[0])
    if scale is not None:
        pair = pair * jnp.asarray(scale, pair.dtype)
    zero = jnp.zeros_like(pair)
    return jnp.where(low_half, pair, zero), jnp.where(low_half, zero, pair)


def attend_forward(proj_ref, ctx_ref, soft_ref, peak_ref, temporal, frames, valid):
    lane = lax.broadcasted_iota(jnp.int32, (8, 128), 1)
    peaks = jnp.full((8, 128), NEGATIVE, F32)
    for block in range(BLOCKS):
        allowed = masks(temporal, block, frames)
        rows = slice(block * CHUNK, (block + 1) * CHUNK)
        row_id = lax.broadcasted_iota(jnp.int32, (CHUNK, 1), 0)
        for pair in range(PAIRS):
            cols = slice(pair * 128, pair * 128 + 128)
            q_a, q_b = split_heads(proj_ref[rows, cols], SCALE)
            keys = proj_ref[rows, D + pair * 128 : D + pair * 128 + 128]
            v_a, v_b = split_heads(proj_ref[rows, 2 * D + pair * 128 : 2 * D + pair * 128 + 128])
            scores = mm_nt(jnp.concatenate([q_a, q_b], axis=0), keys)
            scores = jnp.where(allowed, scores, NEGATIVE)
            top = jnp.max(scores, axis=1, keepdims=True)
            expo = jnp.exp(scores - top)
            total = jnp.sum(expo, axis=1, keepdims=True)
            soft = (expo / total).astype(BF)
            soft_ref[block * PAIRS + pair] = soft
            ctx_ref[rows, cols] = (mm(soft[:CHUNK], v_a) + mm(soft[CHUNK:], v_b)).astype(BF)
            for side in range(2):
                seen = jnp.where(row_id < valid[block], top[side * CHUNK : (side + 1) * CHUNK], NEGATIVE)
                best = jnp.max(seen, axis=0, keepdims=True)
                peaks = jnp.where(lane == 2 * pair + side, jnp.maximum(peaks, best), peaks)
    peak_ref[...] = peaks


def attend_backward(proj_ref, soft_ref, gctx_ref, gproj_ref):
    for block in range(BLOCKS):
        rows = slice(block * CHUNK, (block + 1) * CHUNK)
        for pair in range(PAIRS):
            cols = slice(pair * 128, pair * 128 + 128)
            kcols = slice(D + pair * 128, D + pair * 128 + 128)
            vcols = slice(2 * D + pair * 128, 2 * D + pair * 128 + 128)
            q_pair = jnp.concatenate(split_heads(proj_ref[rows, cols], SCALE), axis=0)
            k_a, k_b = split_heads(proj_ref[rows, kcols], SCALE)
            values = proj_ref[rows, vcols]
            g_pair = jnp.concatenate(split_heads(gctx_ref[rows, cols]), axis=0)
            soft_low = soft_ref[block * PAIRS + pair]
            soft = soft_low.astype(F32)
            grad_soft = mm_nt(g_pair, values)
            inner = jnp.sum(soft * grad_soft, axis=1, keepdims=True)
            grad_scores = (soft * (grad_soft - inner)).astype(BF)
            gproj_ref[rows, cols] = (mm(grad_scores[:CHUNK], k_a) + mm(grad_scores[CHUNK:], k_b)).astype(BF)
            gproj_ref[rows, kcols] = mm_tn(grad_scores, q_pair).astype(BF)
            gproj_ref[rows, vcols] = mm_tn(soft_low, g_pair).astype(BF)


def blocks_between(slot_ref, arrays, plan, weight_ref):
    for array, index, row, column, height, width, place, scale, first, at in plan:
        start = pl.multiple_of(slot_ref[place] * scale + first, 16)
        yield (
            arrays[array].at[index, row : row + height, column : column + width],
            weight_ref.at[pl.ds(start, height), at : at + width],
        )


def fetch(slot_ref, pieces, plan, weight_ref, sems):
    copies = []
    for number, (piece, part) in enumerate(blocks_between(slot_ref, pieces, plan, weight_ref)):
        copies.append(pltpu.make_async_copy(piece, part, sems.at[number]))
        copies[-1].start()
    return copies


def deliver(slot_ref, weight_ref, targets, plan, sems):
    copies = []
    for number, (piece, part) in enumerate(blocks_between(slot_ref, targets, plan, weight_ref)):
        copies.append(pltpu.make_async_copy(part, piece, sems.at[number]))
        copies[-1].start()
    return copies


def take(refs, plan):
    count = 1 + max(entry[0] for entry in plan)
    return refs[:count], refs[count:]


def finish(copies):
    for copy in copies:
        copy.wait()


def project(na_ref, qkv_ref, qv, proj_ref):
    for part in range(3):
        cols = slice(part * D, (part + 1) * D)
        value = mm(na_ref[...], qkv_ref[:, cols])
        if part != 1:
            at = 0 if part == 0 else D
            value = value + qv[:, at : at + D]
        proj_ref[:, cols] = value.astype(BF)


def pad_frames(tok_ref, rows_ref):
    count = tok_ref.shape[0]
    flat = tok_ref[...].astype(F32)
    rows_ref[0:count, :] = flat
    rows_ref[CHUNK : CHUNK + PATCHES, :] = flat[PATCHES:, :]
    rows_ref[PATCHES:CHUNK, :] = jnp.zeros((CHUNK - PATCHES, D), F32)
    rows_ref[CHUNK + PATCHES :, :] = jnp.zeros((CHUNK - PATCHES, D), F32)


def space_forward_kernel(plan, seq, slot_ref, tok_ref, vec_ref, qv_ref, *refs):
    pieces, refs = take(refs, plan)
    part_refs, refs = refs[:seq], refs[seq:]
    na_ref, proj_ref, soft_ref, ctx_ref, peak_ref, rows_ref, weight_ref, sems = refs
    copies = fetch(slot_ref, pieces, plan, weight_ref, sems)
    pad_frames(tok_ref, rows_ref)
    unit, _ = row_stats(rows_ref[...])
    na_ref[...] = (unit * vec_ref[0:1] + vec_ref[3:4]).astype(BF)
    finish(copies)
    project(na_ref, weight_ref, qv_ref[0:1], proj_ref)
    attend_forward(proj_ref, ctx_ref, soft_ref, peak_ref, False, 0, (PATCHES, PATCHES))
    rows_ref[...] = rows_ref[...] + mm(ctx_ref[...], weight_ref[:, 3 * D :]) + vec_ref[6:7]
    frames, width = part_refs[0].shape[0], part_refs[0].shape[1]

    def body(place):
        for distance in range(seq):
            for frame in range(frames):
                start = frame * CHUNK + (place ^ distance) * width
                part_refs[distance][frame] = rows_ref[start : start + width, :].astype(BF)

    for_place(slot_ref, seq, body)


def for_place(slot_ref, count, body):
    for place in range(count):
        pl.when(slot_ref[slot_ref.shape[0] - 1] == place)(functools.partial(body, place))


def interleave(slot_ref, part_refs, stripes_ref, rows_ref):
    shares, frames, width = len(part_refs), part_refs[0].shape[0], part_refs[0].shape[1]
    total = shares * frames
    place = slot_ref[slot_ref.shape[0] - 1]
    for stripe in range(D // 128):
        cols = slice(stripe * 128, stripe * 128 + 128)
        for distance in range(shares):
            for frame in range(frames):
                first = (place ^ distance) * frames + frame
                stripes_ref[stripe, pl.ds(first, width, stride=total), :] = part_refs[distance][frame, :, cols].astype(F32)
        stripes_ref[stripe, total * width :, :] = jnp.zeros((ROWS - total * width, 128), F32)
        rows_ref[:, cols] = stripes_ref[stripe].astype(rows_ref.dtype)


def separate(slot_ref, rows, stripes_ref, part_refs):
    shares, frames, width = len(part_refs), part_refs[0].shape[0], part_refs[0].shape[1]
    total = shares * frames
    place = slot_ref[slot_ref.shape[0] - 1]
    for stripe in range(D // 128):
        cols = slice(stripe * 128, stripe * 128 + 128)
        stripes_ref[stripe] = rows[:, cols]
        for distance in range(shares):
            for frame in range(frames):
                first = (place ^ distance) * frames + frame
                part_refs[distance][frame, :, cols] = stripes_ref[stripe, pl.ds(first, width, stride=total), :].astype(
                    part_refs[distance].dtype
                )


def time_forward_kernel(plan, seq, slot_ref, vec_ref, qv_ref, *refs):
    part_refs, refs = refs[:seq], refs[seq:]
    pieces, refs = take(refs, plan)
    x1_ref, x2_ref, na_ref, proj_ref, soft_ref, ctx_ref, peak_ref, stripes_ref, weight_ref, sems = refs
    copies = fetch(slot_ref, pieces, plan, weight_ref, sems)
    frames = seq * part_refs[0].shape[0]
    count = frames * part_refs[0].shape[1]
    interleave(slot_ref, part_refs, stripes_ref, x1_ref)
    unit, _ = row_stats(x1_ref[...])
    na_ref[...] = (unit * vec_ref[1:2] + vec_ref[4:5]).astype(BF)
    finish(copies)
    project(na_ref, weight_ref, qv_ref[1:2], proj_ref)
    attend_forward(proj_ref, ctx_ref, soft_ref, peak_ref, True, frames, (CHUNK, count - CHUNK))
    x2_ref[...] = x1_ref[...] + mm(ctx_ref[...], weight_ref[:, 3 * D :]) + vec_ref[7:8]


def mlp_kernel(seq, in_plan, out_plan, in_targets, out_targets, slot_ref, x2_ref, vec_ref, inb_ref, *refs):
    gy_refs, refs = refs[:seq], refs[seq:]
    in_pieces, refs = take(refs, in_plan)
    out_pieces, refs = take(refs, out_plan)
    ginb_ref, goutb_ref, *refs = refs
    mixed_refs, refs = refs[:seq], refs[seq:]
    g2_ref, ggain_ref, gshift_ref, *refs = refs
    gin_arrays, refs = take(refs, in_targets)
    gout_arrays, refs = take(refs, out_targets)
    (
        n2_ref, gyl_ref, rows_ref, back_ref, stripes_ref, in_ref, out_ref, gin_ref, gout_ref,
        in_sems, out_sems, gin_sems, gout_sems,
    ) = refs
    blocks = in_ref.shape[1] // FF_BLOCK
    out_height = out_plan[0][4]
    rows_each = FF_BLOCK // out_height

    def span_of(step):
        return pl.ds(pl.multiple_of(step * FF_BLOCK, FF_BLOCK), FF_BLOCK)

    def in_copies(step):
        return [
            pltpu.make_async_copy(piece.at[:, span_of(step)], part.at[:, span_of(step)], in_sems.at[step, number])
            for number, (piece, part) in enumerate(blocks_between(slot_ref, in_pieces, in_plan, in_ref))
        ]

    def gin_copies(step):
        return [
            pltpu.make_async_copy(part.at[:, span_of(step)], piece.at[:, span_of(step)], gin_sems.at[step, number])
            for number, (piece, part) in enumerate(blocks_between(slot_ref, gin_arrays, in_targets, gin_ref))
        ]

    def first_row(entry):
        return slot_ref[entry[6]] * entry[7] + entry[8]

    for step in range(blocks):
        for copy in in_copies(step):
            copy.start()
        if step == 0:
            for entry, (piece, part) in zip(out_plan, blocks_between(slot_ref, out_pieces, out_plan, out_ref)):
                pltpu.make_async_copy(piece, part, out_sems.at[first_row(entry) // out_height]).start()
    unit, _ = row_stats(x2_ref[...])
    n2_ref[...] = (unit * vec_ref[2:3] + vec_ref[5:6]).astype(BF)
    interleave(slot_ref, gy_refs, stripes_ref, gyl_ref)
    goutb_ref[...] = column_sum(gyl_ref[...])
    rows_ref[...] = jnp.zeros_like(rows_ref)
    back_ref[...] = jnp.zeros_like(back_ref)
    gout_copies = [
        pltpu.make_async_copy(part, piece, gout_sems.at[number])
        for number, (piece, part) in enumerate(blocks_between(slot_ref, gout_arrays, out_targets, gout_ref))
    ]

    @pl.loop(0, blocks)
    def _(step):
        span = span_of(step)
        for copy in in_copies(step):
            copy.wait()
        for number in range(rows_each):
            part = out_ref.at[0:out_height, :]
            pltpu.make_async_copy(part, part, out_sems.at[step * rows_each + number]).wait()
        hidden = mm(n2_ref[...], in_ref[:, span]) + inb_ref[:, span]
        cumulative = 0.5 * (1.0 + lax.erf(hidden * (2.0 ** -0.5)))
        act = (hidden * cumulative).astype(BF)
        slope = cumulative + hidden * jnp.exp(-0.5 * hidden * hidden) * 0.3989422804014327
        rows_ref[...] += mm(act, out_ref[span, :])
        gout_ref[span, :] = mm_tn(act, gyl_ref[...]).astype(BF)
        for copy, entry in zip(gout_copies, out_targets):
            pl.when(first_row(entry) // FF_BLOCK == step)(copy.start)
        ghid = (mm_nt(gyl_ref[...], out_ref[span, :]) * slope).astype(BF)
        ginb_ref[:, span] = column_sum(ghid)
        gin_ref[:, span] = mm_tn(n2_ref[...], ghid).astype(BF)
        for copy in gin_copies(step):
            copy.start()
        back_ref[...] += mm_nt(ghid, in_ref[:, span])

    separate(slot_ref, x2_ref[...] + rows_ref[...] + vec_ref[8:9], stripes_ref, mixed_refs)
    unit, inverse = row_stats(x2_ref[...])
    grad = back_ref[...]
    ggain_ref[...] = column_sum(grad * unit)
    gshift_ref[...] = column_sum(grad)
    g2_ref[...] = gyl_ref[...].astype(F32) + norm_backward(grad, unit, inverse, vec_ref[2:3])
    for step in range(blocks):
        finish(gin_copies(step))
    finish(gout_copies)


def branch_backward(g_ref, proj_ref, soft_ref, weight_ref, goutb_ref, gproj_ref, gqv_ref, gbr_ref, gctx_ref):
    gbr_ref[...] = g_ref[...].astype(BF)
    goutb_ref[...] = column_sum(gbr_ref[...])
    gctx_ref[...] = mm_nt(gbr_ref[...], weight_ref[:, 3 * D :]).astype(BF)
    attend_backward(proj_ref, soft_ref, gctx_ref, gproj_ref)
    gqv_ref[:, 0:D] = column_sum(gproj_ref[:, 0:D])
    gqv_ref[:, D:] = column_sum(gproj_ref[:, 2 * D :])


def projection_backward(gproj_ref, weight_ref):
    total = mm_nt(gproj_ref[:, 0:D], weight_ref[:, 0:D])
    for part in range(1, 3):
        cols = slice(part * D, (part + 1) * D)
        total = total + mm_nt(gproj_ref[:, cols], weight_ref[:, cols])
    return total


def weight_grads(na_ref, gproj_ref, ctx_ref, gbr_ref, grad_ref):
    grad_ref[:, 3 * D :] = mm_tn(ctx_ref[...], gbr_ref[...]).astype(BF)
    for part in range(3):
        cols = slice(part * D, (part + 1) * D)
        grad_ref[:, cols] = mm_tn(na_ref[...], gproj_ref[:, cols]).astype(BF)


def time_backward_kernel(plan, seq, slot_ref, g_ref, x1_ref, vec_ref, proj_ref, soft_ref, *refs):
    pieces, refs = take(refs, plan)
    part_refs, refs = refs[:seq], refs[seq:]
    gproj_ref, gbr_ref, goutb_ref, gqv_ref, ggain_ref, gshift_ref, gctx_ref, stripes_ref, weight_ref, sems = refs
    finish(fetch(slot_ref, pieces, plan, weight_ref, sems))
    branch_backward(g_ref, proj_ref, soft_ref, weight_ref, goutb_ref, gproj_ref, gqv_ref, gbr_ref, gctx_ref)
    grad = projection_backward(gproj_ref, weight_ref)
    unit, inverse = row_stats(x1_ref[...])
    ggain_ref[...] = column_sum(grad * unit)
    gshift_ref[...] = column_sum(grad)
    separate(slot_ref, g_ref[...] + norm_backward(grad, unit, inverse, vec_ref[1:2]), stripes_ref, part_refs)


def weight_grad_kernel(targets, slot_ref, na_ref, gproj_ref, ctx_ref, gbr_ref, *refs):
    outs, (grad_ref, sems) = take(refs, targets)
    weight_grads(na_ref, gproj_ref, ctx_ref, gbr_ref, grad_ref)
    finish(deliver(slot_ref, grad_ref, outs, targets, sems))


def space_backward_kernel(plan, targets, seq, slot_ref, na_ref, ctx_ref, proj_ref, soft_ref, *refs):
    part_refs, refs = refs[:seq], refs[seq:]
    pieces, refs = take(refs, plan)
    g_ref, gproj_ref, goutb_ref, gqv_ref = refs[:4]
    outs, refs = take(refs[4:], targets)
    gbr_ref, gctx_ref, weight_ref, grad_ref, sems, grad_sems = refs
    copies = fetch(slot_ref, pieces, plan, weight_ref, sems)
    frames, width = part_refs[0].shape[0], part_refs[0].shape[1]

    def body(place):
        for frame in range(frames):
            for distance in range(seq):
                start = frame * CHUNK + (place ^ distance) * width
                g_ref[start : start + width, :] = part_refs[distance][frame].astype(F32)

    for_place(slot_ref, seq, body)
    for frame in range(frames):
        g_ref[frame * CHUNK + PATCHES : (frame + 1) * CHUNK, :] = jnp.zeros((CHUNK - PATCHES, D), F32)
    finish(copies)
    branch_backward(g_ref, proj_ref, soft_ref, weight_ref, goutb_ref, gproj_ref, gqv_ref, gbr_ref, gctx_ref)
    weight_grads(na_ref, gproj_ref, ctx_ref, gbr_ref, grad_ref)
    finish(deliver(slot_ref, grad_ref, outs, targets, grad_sems))


def space_input_kernel(plan, slot_ref, tok_ref, g_ref, vec_ref, gproj_ref, *refs):
    pieces, refs = take(refs, plan)
    gtok_ref, ggain_ref, gshift_ref, rows_ref, weight_ref, sems = refs
    copies = fetch(slot_ref, pieces, plan, weight_ref, sems)
    pad_frames(tok_ref, rows_ref)
    unit, inverse = row_stats(rows_ref[...])
    finish(copies)
    grad = projection_backward(gproj_ref, weight_ref)
    ggain_ref[...] = column_sum(grad * unit)
    gshift_ref[...] = column_sum(grad)
    rows_ref[...] = g_ref[...] + norm_backward(grad, unit, inverse, vec_ref[0:1])
    gtok_ref[0:PATCHES, :] = rows_ref[0:PATCHES, :]
    gtok_ref[PATCHES:, :] = rows_ref[CHUNK : CHUNK + PATCHES, :]


def call(kernel, outs, scratch, flops, slot, operands, pieces=(), targets=(), sems=(), *, name):
    whole = pl.BlockSpec(memory_space=pltpu.VMEM)
    far = pl.BlockSpec(memory_space=pl.ANY)
    return pl.pallas_call(
        kernel,
        in_specs=[pl.BlockSpec(memory_space=pltpu.SMEM)] + [whole] * len(operands) + [far] * len(pieces),
        out_specs=[whole] * len(outs) + [far] * len(targets),
        out_shape=[jax.ShapeDtypeStruct(shape, dtype) for shape, dtype in list(outs) + list(targets)],
        scratch_shapes=[pltpu.VMEM(shape, dtype) for shape, dtype in scratch]
        + [pltpu.SemaphoreType.DMA(count if isinstance(count, tuple) else (count,)) for count in sems],
        compiler_params=pltpu.CompilerParams(vmem_limit_bytes=VMEM_LIMIT),
        cost_estimate=pl.CostEstimate(flops=COST, bytes_accessed=COST, transcendentals=0),
        name=name,
    )(slot, *operands, *pieces)


def hop(value, axis, bit):
    return lax.ppermute(value, axis, [(index, index ^ bit) for index in range(lax.axis_size(axis))])


CORE, CHIP_X, CHIP_Y = 1, 2, 4
X_ORDER = (0, CHIP_Y, CHIP_X, CHIP_X | CHIP_Y)
Y_ORDER = (0, CHIP_X, CHIP_Y, CHIP_X | CHIP_Y)


def pack_rows(value):
    return jnp.concatenate(jnp.split(value, 4, axis=0), axis=1)


def unpack_rows(value):
    return jnp.concatenate(jnp.split(value, 4, axis=1), axis=0)


def targets_of(height, width, order):
    return [
        (side, chip, 0, 0, height, width, order[chip] ^ shift, height, 0, 0)
        for side, shift in enumerate((0, CORE)) for chip in range(4)
    ]


def gather_plain(own):
    full = lax.all_gather(own[None], "fsdp", axis=1, tiled=True)
    return [full], plain_plan(full.shape[1], full.shape[2])


def plain_plan(rows, columns):
    return [(0, 0, 0, 0, rows, columns, 0, 0, 0, 0)]


tie = lax.optimization_barrier


def sums_of(keep, got):
    return lambda part: keep[part].astype(F32) + got[part].astype(F32)


def pair_of(keep, got, first):
    return sums_of(keep, got)(slice(first + 2, first + 4)).astype(BF)


def rest_of(keep, got, first, came):
    return (sums_of(keep, got)(first + 1) + came[1].astype(F32)).astype(BF)


def own_of(keep, got, first, came, last):
    return sums_of(keep, got)(first) + came[0].astype(F32) + last.astype(F32)


def over_x(value):
    return hop(value, "fsdp", CHIP_X)


def over_y(value):
    return hop(value, "fsdp", CHIP_Y)


def over_core(value):
    return hop(value, "fsdp", CORE)


def reduce_plain(grad):
    return lax.psum_scatter(grad[0], "fsdp", scatter_dimension=0, tiled=True).astype(F32)


def seq_first(value):
    odd = (lax.axis_index("seq") & 1) == 1
    half = value.shape[0] // 2
    low, high = value[:half], value[half:]
    return (jnp.where(odd, high, low) + hop(jnp.where(odd, low, high).astype(BF), "seq", 1).astype(F32)).astype(BF)


def seq_second(part):
    return (part.astype(F32) + hop(part, "seq", 2).astype(F32)).astype(BF)


def seq_third(part):
    odd = (lax.axis_index("seq") & 1) == 1
    other = hop(part, "seq", 1)
    return jnp.where(odd, jnp.concatenate([other, part]), jnp.concatenate([part, other])).astype(F32)


def seq_total(value):
    if lax.axis_size("seq") != 4:
        return lax.psum(value.astype(BF), "seq").astype(F32)
    return seq_third(seq_second(seq_first(value)))


def by_distance(parts, place):
    shape = parts.shape
    bit = 1
    while bit < shape[0]:
        paired = parts.reshape((shape[0] // (2 * bit), 2, bit) + shape[1:])
        parts = jnp.where((place & bit) != 0, paired[:, ::-1], paired).reshape(shape)
        bit *= 2
    return parts


def swap(parts):
    return [parts[0]] + [hop(parts[distance], "seq", distance) for distance in range(1, len(parts))]


def on_device(
    tokens, norm_gain, norm_bias, attn_qkv, attn_qv_bias, attn_out, attn_out_bias,
    mlp_in, mlp_in_bias, mlp_out, mlp_out_bias, threshold, cotangent,
):
    clip_count, local_len, _ = tokens.shape
    seq, shards = lax.axis_size("seq"), lax.axis_size("fsdp")
    me = lax.axis_index("fsdp")
    frames = local_len // PATCHES
    width = PATCHES // seq
    own_rows = D // shards
    ff = mlp_in.shape[1]
    split_shape = (seq, frames, width, D)
    tok = tokens.reshape(local_len, D)
    cot = jnp.swapaxes(cotangent.reshape(frames, seq, width, D), 0, 1)
    by_chip = shards == 8

    attn_own = [jnp.concatenate([attn_qkv[a], attn_out[a]], axis=1) for a in range(2)]
    small = jnp.concatenate([
        norm_gain, norm_bias, attn_out_bias, mlp_out_bias.reshape(1, own_rows), attn_qv_bias.reshape(-1, own_rows),
        mlp_in_bias.reshape(-1, own_rows),
    ])
    place = lax.axis_index("seq")
    half = own_rows // 2
    ff_rows = ff // D
    if by_chip:
        slot = me ^ jnp.arange(shards, dtype=jnp.int32)
        low, high = attn_own[0][:half], attn_own[0][half:]
        near_x, near_y = jnp.stack([low, over_x(low)]), jnp.stack([high, over_y(high)])
        core_x, core_y = over_core(near_x), over_core(near_y)
        core_x, core_y, small = tie((core_x, core_y, small))
        small = jnp.stack([small, over_x(small), over_y(small), hop(small, "fsdp", CHIP_X | CHIP_Y)])
        far_x, far_y = over_y(near_x), over_x(near_y)
        small = jnp.stack([small, over_core(small)], axis=1).reshape((shards,) + small.shape[1:])
        small = by_distance(small, me)
        low, high = attn_own[1][:half], attn_own[1][half:]
        first_x, first_y, first_out = jnp.concatenate([low, mlp_in]), high, mlp_out
        far_x, far_y, core_x, core_y, first_x, first_y, first_out = tie(
            (far_x, far_y, core_x, core_y, first_x, first_y, first_out)
        )
        first_x, first_y, first_out = over_x(first_x), over_y(first_y), over_y(first_out)
        space_w = [near_x, far_x, near_y, far_y, core_x, over_core(far_x), core_y, over_core(far_y)]
        places = ((0, CHIP_X), (CHIP_Y, CHIP_X | CHIP_Y), (0, CHIP_Y), (CHIP_X, CHIP_X | CHIP_Y))
        attn_plan, in_plan, out_plan, out_rows = [], [], [], mlp_out.shape[0]
        for array in range(8):
            shift, lower = (0 if array < 4 else CORE), array % 4 < 2
            for index, owner in enumerate(places[array % 4]):
                owner = owner ^ shift
                attn_plan.append((array, index, 0, 0, half, 4 * D, owner, own_rows, 0 if lower else half, 0))
                array_of = array % 2 + (0 if array < 4 else 2)
                if lower:
                    in_plan.append((array_of, index, 0, 0, own_rows, ff, owner, own_rows, 0, 0))
                else:
                    out_plan.append((array_of, index, 0, 0, out_rows, D, owner, out_rows, 0, 0))
        in_targets, out_targets = targets_of(own_rows, ff, X_ORDER), targets_of(out_rows, D, Y_ORDER)
        in_shapes, out_shapes = [((4, own_rows, ff), BF)] * 2, [((4, out_rows, D), BF)] * 2
        attn_targets = [
            (side, 4 * lower + chip, 0, 0, half, 4 * D, (X_ORDER, Y_ORDER)[lower][chip] ^ shift, own_rows, lower * half, 0)
            for side, shift in enumerate((0, CORE)) for lower in range(2) for chip in range(4)
        ]
        attn_shapes = [((8, half, 4 * D), BF)] * 2
    else:
        slot = jnp.zeros((1,), jnp.int32)
        small = lax.all_gather(small, "fsdp", axis=0)
        space_w, attn_plan = gather_plain(attn_own[0])
        time_w, _ = gather_plain(attn_own[1])
        in_w, in_plan = gather_plain(mlp_in)
        out_w, _ = gather_plain(mlp_out)
        out_plan = [(0, 0, row, 0, FF_BLOCK, D, 0, 0, row, 0) for row in range(0, ff, FF_BLOCK)]
        in_targets, out_targets = plain_plan(D, ff), out_plan
        in_shapes, out_shapes = [((1, D, ff), BF)], [((1, ff, D), BF)]
        attn_targets, attn_shapes = plain_plan(D, 4 * D), [((1, D, 4 * D), BF)]
    slot = jnp.concatenate([slot, place[None]])
    small = small.astype(F32)
    turned = by_distance(cot, place)
    gy = [turned[distance] for distance in range(seq)]

    def spread(first, count, inner):
        rows = small[:, first : first + count * inner].reshape(shards, count, inner, own_rows)
        return jnp.swapaxes(rows, 0, 1).reshape(count, shards * inner * own_rows)

    vectors = spread(0, 9, 1)
    qv, inb = spread(9, 2, 2), spread(13, 1, ff_rows)

    state = [
        ((ROWS, D), BF), ((ROWS, 3 * D), BF), ((BLOCKS * PAIRS, 2 * CHUNK, CHUNK), BF), ((ROWS, D), BF), ((8, 128), F32),
    ]
    shares = [(split_shape[1:], BF)] * seq
    weight = ((D, 4 * D), BF)
    stripes = ((D // 128, ROWS, 128), F32)
    attn_flops = 2 * ROWS * D * 4 * D + 4 * BLOCKS * H * CHUNK * CHUNK * HD
    line = lambda cols: ((1, cols), F32)

    *parts, na0, proj0, soft0, ctx0, peak0 = call(
        functools.partial(space_forward_kernel, attn_plan, seq), shares + state, [((ROWS, D), F32), weight],
        attn_flops, slot, (tok, vectors, qv), space_w, sems=(len(attn_plan),), name="space_forward",
    )
    parts = swap(parts)
    if by_chip:
        na0, first_x, first_y, first_out = tie((na0, first_x, first_y, first_out))
        near_x, near_y = jnp.stack([low, first_x[:half]]), jnp.stack([high, first_y])
        far_x, far_y = over_y(near_x), over_x(near_y)
        in_near, out_near = jnp.stack([mlp_in, first_x[half:]]), jnp.stack([mlp_out, first_out])
        parts, near_x, near_y, far_x, far_y, in_near, out_near = tie((parts, near_x, near_y, far_x, far_y, in_near, out_near))
        time_w = [near_x, far_x, near_y, far_y] + [over_core(piece) for piece in (near_x, far_x, near_y, far_y)]
        in_far, out_far = over_y(in_near), over_x(out_near)
        parts, gy = tie((parts, gy))
    gy = swap(gy)
    x1, x2, na1, proj1, soft1, ctx1, peak1 = call(
        functools.partial(time_forward_kernel, attn_plan, seq), [((ROWS, D), F32), ((ROWS, D), F32)] + state,
        [stripes, weight], attn_flops, slot, [vectors, qv] + parts, time_w, sems=(len(attn_plan),), name="time_forward",
    )
    if by_chip:
        in_core, out_core = over_core(in_near), over_core(out_near)
        x2, gy, in_core, out_core = tie((x2, gy, in_core, out_core))
        in_w = [in_near, in_far, in_core, over_core(in_far)]
        out_w = [out_near, out_far, out_core, over_core(out_far)]

    ginb, g_moutb, *results = call(
        functools.partial(mlp_kernel, seq, in_plan, out_plan, in_targets, out_targets),
        [line(ff), line(D)] + shares + [((ROWS, D), F32), line(D), line(D)],
        [((ROWS, D), BF)] * 2 + [((ROWS, D), F32)] * 2 + [stripes] + [((D, ff), BF), ((ff, D), BF)] * 2,
        10 * ROWS * D * ff, slot, [x2, vectors, inb] + gy, in_w + out_w, in_shapes + out_shapes,
        ((ff // FF_BLOCK, len(in_plan)), len(out_plan), (ff // FF_BLOCK, len(in_targets)), len(out_targets)), name="mlp",
    )
    mixed, (g2, ggain2, gshift2, *mlp_grads) = results[:seq], results[seq:]
    in_grads, out_grads = mlp_grads[: len(in_shapes)], mlp_grads[len(in_shapes) :]

    if by_chip:
        (in_keep, in_send), (out_keep, out_send) = in_grads, out_grads
        in_got, out_got = over_core(in_send), over_core(out_send)
        in_pair, out_pair = pair_of(in_keep, in_got, 0), pair_of(out_keep, out_got, 0)
        g2, in_pair, out_pair, mixed = tie((g2, in_pair, out_pair, mixed))
        in_came, out_came = over_x(in_pair), over_y(out_pair)
    mixed = swap(mixed)
    *parts, gproj1, gbr1, g_outb1, g_qv1, ggain1, gshift1 = call(
        functools.partial(time_backward_kernel, attn_plan, seq),
        shares + [((ROWS, 3 * D), BF), ((ROWS, D), BF), line(D), line(2 * D), line(D), line(D)],
        [((ROWS, D), BF), stripes, weight], 2 * attn_flops,
        slot, (g2, x1, vectors, proj1, soft1), time_w, sems=(len(attn_plan),), name="time_backward",
    )
    if by_chip:
        parts, mixed = tie((parts, mixed))
    parts = swap(parts)
    time_grads = call(
        functools.partial(weight_grad_kernel, attn_targets), [], [weight], attn_flops,
        slot, (na1, gproj1, ctx1, gbr1), (), attn_shapes, (len(attn_targets),), name="time_weight_grad",
    )
    if by_chip:
        time_keep, time_send = time_grads
        in_rest, out_rest = rest_of(in_keep, in_got, 0, in_came), rest_of(out_keep, out_got, 0, out_came)
        parts, time_send, in_rest, out_rest = tie((parts, time_send, in_rest, out_rest))
        time_got = over_core(time_send)
        in_last, out_last = over_y(in_rest), over_x(out_rest)
        time_pairs = pair_of(time_keep, time_got, 0), pair_of(time_keep, time_got, 4)
        soft0, time_pairs = tie((soft0, time_pairs))
        time_came = over_x(time_pairs[0]), over_y(time_pairs[1])
    g1, gproj0, g_outb0, g_qv0, *space_grads = call(
        functools.partial(space_backward_kernel, attn_plan, attn_targets, seq),
        [((ROWS, D), F32), ((ROWS, 3 * D), BF), line(D), line(2 * D)],
        [((ROWS, D), BF), ((ROWS, D), BF), weight, weight], 2 * attn_flops,
        slot, [na0, ctx0, proj0, soft0] + parts, space_w, attn_shapes, (len(attn_plan), len(attn_targets)),
        name="space_backward",
    )
    if by_chip:
        space_keep, space_send = space_grads
        space_send, time_came, in_last, out_last = tie((space_send, time_came, in_last, out_last))
        space_got = over_core(space_send)
        mlp_total = jnp.concatenate([
            own_of(in_keep, in_got, 0, in_came, in_last), pack_rows(own_of(out_keep, out_got, 0, out_came, out_last)),
        ])
        time_rests = rest_of(time_keep, time_got, 0, time_came[0]), rest_of(time_keep, time_got, 4, time_came[1])
        space_pairs = pair_of(space_keep, space_got, 0), pair_of(space_keep, space_got, 4)
        g1, mlp_total, time_rests, space_pairs = tie((g1, mlp_total, time_rests, space_pairs))
        mlp_part = seq_first(mlp_total)
        time_lasts = over_y(time_rests[0]), over_x(time_rests[1])
        space_came = over_x(space_pairs[0]), over_y(space_pairs[1])
    g_tok, ggain0, gshift0 = call(
        functools.partial(space_input_kernel, attn_plan), [((local_len, D), F32), line(D), line(D)],
        [((ROWS, D), F32), weight], attn_flops,
        slot, (tok, g1, vectors, gproj0), space_w, sems=(len(attn_plan),), name="space_input",
    )

    def gathered(value, inner):
        count = value.shape[0]
        return jnp.swapaxes(value.reshape(count, shards, inner, own_rows), 0, 1).reshape(shards, count * inner, own_rows)

    if by_chip:
        (ggain0, ggain1, ggain2, gshift0, gshift1, gshift2, g_outb0, g_outb1, g_moutb, g_qv0, g_qv1, ginb, mlp_part) = tie(
            (ggain0, ggain1, ggain2, gshift0, gshift1, gshift2, g_outb0, g_outb1, g_moutb, g_qv0, g_qv1, ginb, mlp_part)
        )
        mlp_part = seq_second(mlp_part)
        ggain0, time_lasts, space_came = tie((ggain0, time_lasts, space_came))
    small_grads = jnp.concatenate([
        gathered(jnp.concatenate([ggain0, ggain1, ggain2, gshift0, gshift1, gshift2, g_outb0, g_outb1, g_moutb]), 1),
        gathered(jnp.concatenate([g_qv0, g_qv1]), 2), gathered(ginb, ff_rows),
    ], axis=1)
    peaks = jnp.concatenate([peak0[0:1], peak1[0:1]], axis=1)
    mine = (jnp.arange(shards * seq) == me * seq + place)[:, None]
    peaks = jnp.where(mine, peaks, 0.0).reshape(-1, 128)
    small_grads = jnp.concatenate([small_grads.reshape(-1, 128), peaks])
    if by_chip:
        space_rests = rest_of(space_keep, space_got, 0, space_came[0]), rest_of(space_keep, space_got, 4, space_came[1])
        space_lasts = over_y(space_rests[0]), over_x(space_rests[1])
        time_total = jnp.concatenate([
            own_of(time_keep, time_got, 0, time_came[0], time_lasts[0]), own_of(time_keep, time_got, 4, time_came[1], time_lasts[1]),
        ])
        time_part = seq_first(time_total)
        small_grads = small_grads + over_core(small_grads)
        space_lasts, time_part, mlp_part, small_grads = tie((space_lasts, time_part, mlp_part, small_grads))
        space_total = jnp.concatenate([
            own_of(space_keep, space_got, 0, space_came[0], space_lasts[0]),
            own_of(space_keep, space_got, 4, space_came[1], space_lasts[1]),
        ])
        space_part = seq_first(space_total)
        small_grads = small_grads + over_x(small_grads)
        small_grads = small_grads + over_y(small_grads)
        time_part = seq_second(time_part)
        space_part, small_grads, mlp_part = tie((space_part, small_grads, mlp_part))
        space_part = seq_second(space_part)
        small_grads = small_grads + hop(small_grads, "seq", 1)
        mlp_total = seq_third(mlp_part)
        space_part, time_part, small_grads = tie((space_part, time_part, small_grads))
        small_grads = small_grads + hop(small_grads, "seq", 2)
        grad_in, grad_mout = mlp_total[:own_rows], unpack_rows(mlp_total[own_rows:])
        attn_totals = [seq_third(space_part), seq_third(time_part)]
    else:
        small_grads = lax.psum(small_grads, ("fsdp", "seq"))
        (in_grads,), (out_grads,) = in_grads, out_grads
        in_total, out_total, time_total, space_total = (
            reduce_plain(value) for value in (in_grads, out_grads, time_grads[0], space_grads[0])
        )
        grad_in, grad_mout = seq_total(in_total), seq_total(out_total)
        attn_totals = [seq_total(space_total), seq_total(time_total)]
    grad_qkv = jnp.stack([value[:, : 3 * D] for value in attn_totals])
    grad_out = jnp.stack([value[:, 3 * D :] for value in attn_totals])

    peaks = small_grads[-peaks.shape[0] :].reshape(shards * seq, 2, 128)
    logit_max = jnp.max(peaks, axis=0)[:, :H]
    small_grads = small_grads[: -2 * shards * seq].reshape(shards, -1, own_rows)
    small_grads = lax.dynamic_index_in_dim(small_grads, me, 0, keepdims=False)
    grad_gain, grad_shift, grad_outb, grad_moutb = small_grads[0:3], small_grads[3:6], small_grads[6:8], small_grads[8]
    grad_qv = small_grads[9:13].reshape(2, 2 * own_rows)
    grad_inb = small_grads[13:].reshape(ff_rows * own_rows)

    factor = threshold / jnp.maximum(logit_max, threshold)
    column_scale = jnp.repeat(jnp.sqrt(factor), HD, axis=1)
    clipped = attn_qkv[:, :, : 2 * D].astype(F32) * jnp.concatenate([column_scale, column_scale], axis=1)[:, None, :]
    mixed = jnp.swapaxes(by_distance(jnp.stack(mixed), place), 0, 1).reshape(tokens.shape)
    return (
        mixed, g_tok.reshape(tokens.shape), grad_gain, grad_shift, grad_qkv, grad_qv, grad_out, grad_outb,
        grad_in, grad_inb, grad_mout, grad_moutb, logit_max, clipped,
    )


def solution(mesh):
    placed = (
        P("fsdp", "seq", None), P(None, "fsdp"), P(None, "fsdp"), P(None, "fsdp", None), P(None, "fsdp"),
        P(None, "fsdp", None), P(None, "fsdp"), P("fsdp", None), P("fsdp"), P("fsdp", None), P("fsdp"), P(),
        P("fsdp", "seq", None),
    )
    return jax.shard_map(
        on_device,
        mesh=mesh,
        in_specs=placed,
        out_specs=(
            P("fsdp", "seq", None), P("fsdp", "seq", None), P(None, "fsdp"), P(None, "fsdp"), P(None, "fsdp", None),
            P(None, "fsdp"), P(None, "fsdp", None), P(None, "fsdp"), P("fsdp", None), P("fsdp"), P("fsdp", None),
            P("fsdp"), P(), P(None, "fsdp", None),
        ),
        check_vma=False,
    )
```

time: 821 us -> 375 us (0.46)
  waiting for transfers between devices: 510 us -> 133 us
  blocking collectives: 153 us -> 0 us
  starting transfers between devices: 15.5 us -> 65.5 us
  other arithmetic: 8.77 us -> 48.6 us
  between operations: 16.8 us -> 2.05 us
  Pallas kernels: 81.6 us -> 94.3 us
    reduce_scatter x6 -> x0, waiting for transfers between devices: 238 us -> none  [scatter(): return lax.psum_scatter(value, 'fsdp', scatter_dimension=axis, tiled=True)]
    ppermute x0 -> x69, waiting for transfers between devices: none -> 133 us  [hop(): lax.ppermute(value, axis, [(index, index ^ bit) for index in range(lax.ax...]
    all_gather x6 -> x0, waiting for transfers between devices: 107 us -> none  [gather(): return lax.all_gather(value, 'fsdp', axis=axis, tiled=True)]
    psum x1 -> x0, waiting for transfers between devices: 86.5 us -> none  [total(): return lax.psum(scatter(value, axis).astype(BF), 'seq').astype(F32)]
    unnamed x21 -> x0, waiting for transfers between devices: 78.9 us -> none
    ppermute x0 -> x69, starting transfers between devices: none -> 65.5 us  [hop(): lax.ppermute(value, axis, [(index, index ^ bit) for index in range(lax.ax...]
    all_gather x5 -> x0, blocking collectives: 43.3 us -> none  [gather(): return lax.all_gather(value, 'fsdp', axis=axis, tiled=True)]
    pmax x1 -> x0, blocking collectives: 39.4 us -> none  [on_device(): logit_max = lax.pmax(peak_pair, ('fsdp', 'seq'))]
  transfers between devices with their start and end apart: 20 -> 69, of which waited for: 13 -> 26; matrix products, arithmetic and copies ran while one was open for 4% -> 16% of each run, Pallas kernels for 5% -> 19%
where the time goes in v2:
time: 375 us; the launch traced here: 368 us
  waiting for transfers between devices  133 us (35%)
  Pallas kernels  94.3 us (25%)
  starting transfers between devices  65.5 us (17%)
  other arithmetic  48.6 us (13%)
  local copies, waits for them, and re-layouts  24.3 us (6%)
    ppermute x69, waiting for transfers between devices, hop(): lax.ppermute(value, axis, [(index, index ^ bit) for index in range(lax.ax...  133 us
    pallas_call x7, Pallas kernels, call(): pl.pallas_call(kernel, in_specs=[pl.BlockSpec(memory_space=pltpu.SMEM)] +...  94.3 us
    ppermute x69, starting transfers between devices, hop(): lax.ppermute(value, axis, [(index, index ^ bit) for index in range(lax.ax...  65.5 us
    convert_element_type x4, other arithmetic, rest_of(): return (sums_of(keep, got)(first + 1) + came[1].astype(F32)).astype(BF)  8.74 us
    convert_element_type x4, other arithmetic, pair_of(): return sums_of(keep, got)(slice(first + 2, first + 4)).astype(BF)  7.63 us
  transfers between devices with their start and end apart: 69, of which 26 were waited for; matrix products, arithmetic and copies ran while one was open for 16% of the time, Pallas kernels for 19%

profile of v2, /device:TPU:0, one launch (start us, length us, event | category | flops | bytes accessed | tf_op | source)
XLA Modules:
  0.0 367.7 jit_solution(9363072967044204324)
XLA Ops:
  7.9 5.1 %collective-permute-done = bf16[48,3072]{1,0:T(8,128)(2,1)S(1)} collective-permute-done((bf16[48,3072]{1,0:T(8,128)(2,1)S(1)}, bf16[48,3072]{1,0:T(8,128)(2,1)S(1)}, u32[]{:S(2)}, u32[]{:S(2)}) %collective-permute-start) | collective-permute-done | bytes 294944 | tf_op jit(solution)/shard_map/ppermute | solution.py:443
  22.9 9.6 %collective-permute-done.6 = bf16[17,96]{1,0:T(8,128)(2,1)S(1)} collective-permute-done((bf16[17,96]{1,0:T(8,128)(2,1)S(1)}, bf16[17,96]{1,0:T(8,128)(2,1)S(1)}, u32[]{:S(2)}, u32[]{:S(2)}) %collective-permute-start.6) | collective-permute-done | bytes 3296 | tf_op jit(solution)/shard_map/ppermute | solution.py:443
  49.3 11.8 %space_forward.1 = (bf16[2,49,768]{2,1,0:T(8,128)(2,1)}, bf16[2,49,768]{2,1,0:T(8,128)(2,1)}, bf16[2,49,768]{2,1,0:T(8,128)(2,1)}, bf16[2,49,768]{2,1,0:T(8,128)...) custom-call(s32[9]{0:T(128)} %pad_add_fusion.slot_ref, ...), custom_call_target="tpu_custom_call" | custom-call | flops 1000 | bytes 1000 | tf_op jit(solution)/shard_map/space_forward/pallas_call | solution.py:429
  72.6 5.9 %collective-permute-done.13.refs_2_ = bf16[2,49,768]{2,1,0:T(8,128)(2,1)S(1)} collective-permute-done((bf16[2,49,768]{2,1,0:T(8,128)(2,1)}, bf16[2,49,768]{2,1,0:T(8,128)(2,1)S(1)}, u32[]{:S(2)}, u32[]{:S(2)}) %collective-permute-start.13) | collective-permute-done | bytes 150560 | tf_op jit(solution)/shard_map/ppermute | solution.py:443
  87.5 5.8 %collective-permute-done.24.refs_1_ = bf16[2,49,768]{2,1,0:T(8,128)(2,1)S(1)} collective-permute-done((bf16[2,49,768]{2,1,0:T(8,128)(2,1)S(1)}, bf16[2,49,768]{2,1,0:T(8,128)(2,1)S(1)}, u32[]{:S(2)}, u32[]{:S(2)}) %collective-permute-start.24) | collective-permute-done | bytes 150560 | tf_op jit(solution)/shard_map/ppermute | solution.py:443
  95.6 8.0 %collective-permute-done.25.refs_2_ = bf16[2,49,768]{2,1,0:T(8,128)(2,1)} collective-permute-done((bf16[2,49,768]{2,1,0:T(8,128)(2,1)S(1)}, bf16[2,49,768]{2,1,0:T(8,128)(2,1)}, u32[]{:S(2)}, u32[]{:S(2)}) %collective-permute-start.25) | collective-permute-done | bytes 150560 | tf_op jit(solution)/shard_map/ppermute | solution.py:443
  104.3 4.4 %collective-permute-done.29.refs_5_ = bf16[2,96,3072]{2,1,0:T(8,128)(2,1)} collective-permute-done((bf16[2,96,3072]{2,1,0:T(8,128)(2,1)S(1)}, bf16[2,96,3072]{2,1,0:T(8,128)(2,1)}, u32[]{:S(2)}, u32[]{:S(2)}) %collective-permute-start.29) | collective-permute-done | bytes 1179680 | tf_op jit(solution)/shard_map/ppermute | solution.py:443
  109.8 3.5 collective-permute-done.23.refs_11_.refs_7_
  113.3 3.5 collective-permute-start.26
  117.5 11.0 %time_forward.1 = (f32[416,768]{1,0:T(8,128)}, f32[416,768]{1,0:T(8,128)}, bf16[416,768]{1,0:T(8,128)(2,1)}, bf16[416,2304]{1,0:T(8,128)(2,1)}, bf16[12,416,208]...) custom-call(s32[9]{0:T(128)} %pad_add_fusion.slot_ref, f32[9,768]{1,0:T(8,128)} %reshape.198.vec_ref, ...), custom_call_target="tpu_custom_call" | custom-call | flops 1000 | bytes 1000 | tf_op jit(solution)/shard_map/time_forward/pallas_call | solution.py:429
  129.1 23.5 %mlp.1 = (f32[1,3072]{1,0:T(1,128)}, f32[1,768]{1,0:T(1,128)}, bf16[2,49,768]{2,1,0:T(8,128)(2,1)}, bf16[2,49,768]{2,1,0:T(8,128)(2,1)}, bf16[2,49,768]{2,1,0:T(...) custom-call(s32[9]{0:T(128)} %pad_add_fusion.slot_ref, ...), custom_call_target="tpu_custom_call" | custom-call | flops 1000 | bytes 1000 | tf_op jit(solution)/shard_map/mlp/pallas_call | solution.py:429
  153.2 4.2 %collective-permute-done.33 = bf16[4,96,3072]{2,1,0:T(8,128)(2,1)S(1)} collective-permute-done((bf16[4,96,3072]{2,1,0:T(8,128)(2,1)}, bf16[4,96,3072]{2,1,0:T(8,128)(2,1)S(1)}, u32[]{:S(2)}, u32[]{:S(2)}) %collective-permute-start.33) | collective-permute-done | bytes 2359328 | tf_op jit(solution)/shard_map/ppermute | solution.py:443
  169.9 15.5 %time_backward.1 = (bf16[2,49,768]{2,1,0:T(8,128)(2,1)}, bf16[2,49,768]{2,1,0:T(8,128)(2,1)}, bf16[2,49,768]{2,1,0:T(8,128)(2,1)}, bf16[2,49,768]{2,1,0:T(8,128)...) custom-call(s32[9]{0:T(128)} %pad_add_fusion.slot_ref, ...), custom_call_target="tpu_custom_call" | custom-call | flops 1000 | bytes 1000 | tf_op jit(solution)/shard_map/time_backward/pallas_call | solution.py:429
  185.3 7.3 %time_weight_grad.1 = (bf16[8,48,3072]{2,1,0:T(8,128)(2,1)}, bf16[8,48,3072]{2,1,0:T(8,128)(2,1)}) custom-call(s32[9]{0:T(128)} %pad_add_fusion.slot_ref, bf16[416,768]{1,0:T(8,128)(2,1)} %get-tuple-element.241.na_ref, bf16[416,2304]{1,0:T(8,128)(2,1)} %get-tuple-element.242.gproj_ref, bf16[416,768]{1,0:T(8,128)(2,1)} %get-tuple-element.243.ctx_ref, ...), custom_call_target="tpu_custom_call" | custom-call | flops 1000 | bytes 1000 | tf_op jit(solution)/shard_map/time_weight_grad/pallas_call | solution.py:429
  193.7 3.5 collective-permute-start.40
  202.1 6.1 %collective-permute-done.39.refs_2_ = bf16[2,49,768]{2,1,0:T(8,128)(2,1)S(1)} collective-permute-done((bf16[2,49,768]{2,1,0:T(8,128)(2,1)}, bf16[2,49,768]{2,1,0:T(8,128)(2,1)S(1)}, u32[]{:S(2)}, u32[]{:S(2)}) %collective-permute-start.39) | collective-permute-done | bytes 150560 | tf_op jit(solution)/shard_map/ppermute | solution.py:443
  215.9 17.6 %space_backward.1 = (f32[416,768]{1,0:T(8,128)}, bf16[416,2304]{1,0:T(8,128)(2,1)}, f32[1,768]{1,0:T(1,128)}, f32[1,1536]{1,0:T(1,128)}, bf16[8,48,3072]{2,1,0:T(8,128)(2,1)}, /*index=5*/bf16[8,48,3072]{2,1,0:T(8,128)(2,1)}) custom-call(s32[9]{0:T(128)} %pad_add_fusion.slot_ref, bf16[416,768]{1,0:T(8,128)(2,1)} %get-tuple-element.237.na_ref, ...), custom_call_target="tpu_custom_call" | custom-call | flops 1000 | bytes 1000 | tf_op jit(solution)/shard_map/space_backward/pallas_call | solution.py:429
  233.5 4.2 %collective-permute-done.44 = bf16[2,48,3072]{2,1,0:T(8,128)(2,1)S(1)} collective-permute-done((bf16[2,48,3072]{2,1,0:T(8,128)(2,1)}, bf16[2,48,3072]{2,1,0:T(8,128)(2,1)S(1)}, u32[]{:S(2)}, u32[]{:S(2)}) %collective-permute-start.44) | collective-permute-done | bytes 589856 | tf_op jit(solution)/shard_map/ppermute | solution.py:443
  254.9 7.7 %space_input.1 = (f32[392,768]{1,0:T(8,128)}, f32[1,768]{1,0:T(1,128)}, f32[1,768]{1,0:T(1,128)}) custom-call(s32[9]{0:T(128)} %pad_add_fusion.slot_ref, bf16[392,768]{1,0:T(8,128)(2,1)} %bitcast.145, f32[416,768]{1,0:T(8,128)} %get-tuple-element.271.g_ref, f32[9,768]{1,0:T(8,128)} %reshape.198.vec_ref, bf16[416,2304]{1,0:T(8,128)(2,1)} %get-tuple-element.272.gproj_ref, ...), custom_call_target="tpu_custom_call" | custom-call | flops 1000 | bytes 1000 | tf_op jit(solution)/shard_map/space_input/pallas_call | solution.py:429
  267.7 5.7 %collective-permute-done.52 = bf16[2,48,3072]{2,1,0:T(8,128)(2,1)} collective-permute-done((bf16[2,48,3072]{2,1,0:T(8,128)(2,1)}, bf16[2,48,3072]{2,1,0:T(8,128)(2,1)}, u32[]{:S(2)}, u32[]{:S(2)}) %collective-permute-start.52) | collective-permute-done | bytes 589856 | tf_op jit(solution)/shard_map/ppermute | solution.py:443
  280.6 17.7 %collective-permute-done.56 = bf16[48,3072]{1,0:T(8,128)(2,1)S(1)} collective-permute-done((bf16[48,3072]{1,0:T(8,128)(2,1)S(1)}, bf16[48,3072]{1,0:T(8,128)(2,1)S(1)}, u32[]{:S(2)}, u32[]{:S(2)}) %collective-permute-start.56) | collective-permute-done | bytes 294944 | tf_op jit(solution)/shard_map/ppermute | solution.py:443
  317.2 11.5 %collective-permute-done.63 = bf16[48,3072]{1,0:T(8,128)(2,1)S(1)} collective-permute-done((bf16[48,3072]{1,0:T(8,128)(2,1)S(1)}, bf16[48,3072]{1,0:T(8,128)(2,1)S(1)}, u32[]{:S(2)}, u32[]{:S(2)}) %collective-permute-start.63) | collective-permute-done | bytes 294944 | tf_op jit(solution)/shard_map/ppermute | solution.py:443
  328.8 4.4 %collective-permute-done.62 = bf16[48,3072]{1,0:T(8,128)(2,1)S(1)} collective-permute-done((bf16[48,3072]{1,0:T(8,128)(2,1)S(1)}, bf16[48,3072]{1,0:T(8,128)(2,1)S(1)}, u32[]{:S(2)}, u32[]{:S(2)}) %collective-permute-start.62) | collective-permute-done | bytes 294944 | tf_op jit(solution)/shard_map/ppermute | solution.py:443
  343.9 18.3 %collective-permute-done.67 = bf16[48,3072]{1,0:T(8,128)(2,1)S(1)} collective-permute-done((bf16[48,3072]{1,0:T(8,128)(2,1)S(1)}, bf16[48,3072]{1,0:T(8,128)(2,1)S(1)}, u32[]{:S(2)}, u32[]{:S(2)}) %collective-permute-start.67) | collective-permute-done | bytes 294944 | tf_op jit(solution)/shard_map/ppermute | solution.py:443
  (360 shorter events, 149.8 us)
Async XLA Ops:
  15.4 24.0 %collective-permute-start.8 = (bf16[2,48,3072]{2,1,0:T(8,128)(2,1)S(1)}, bf16[2,48,3072]{2,1,0:T(8,128)(2,1)S(1)}, u32[]{:S(2)}, u32[]{:S(2)}) collective-permute-start(bf16[2,48,3072]{2,1,0:T(8,128)(2,1)S(1)} %pad_maximum_fusion.6.refs_0_.refs_4_), channel_id=1, source_target_pairs={{0,16},{4,20},{8,24},{12,28},{16,0},{20,4},{24,8},{28,12},{1,17},{... | collective-permute-start | bytes 1769480 | tf_op jit(solution)/shard_map/ppermute | solution.py:443
  16.9 22.5 %collective-permute-start.9 = (bf16[2,48,3072]{2,1,0:T(8,128)(2,1)S(1)}, bf16[2,48,3072]{2,1,0:T(8,128)(2,1)S(1)}, u32[]{:S(2)}, u32[]{:S(2)}) collective-permute-start(bf16[2,48,3072]{2,1,0:T(8,128)(2,1)S(1)} %pad_maximum_fusion.7.refs_2_.refs_6_), channel_id=1, source_target_pairs={{0,8},{4,12},{8,0},{12,4},{16,24},{20,28},{24,16},{28,20},{1,9},{5... | collective-permute-start | bytes 1769480 | tf_op jit(solution)/shard_map/ppermute | solution.py:443
  39.5 25.9 %collective-permute-start.16 = (bf16[48,3072]{1,0:T(8,128)(2,1)}, bf16[48,3072]{1,0:T(8,128)(2,1)S(1)}, u32[]{:S(2)}, u32[]{:S(2)}) collective-permute-start(bf16[48,3072]{1,0:T(8,128)(2,1)} %get-tuple-element.181), channel_id=1, source_target_pairs={{0,16},{4,20},{8,24},{12,28},{16,0},{20,4},{24,8},{28,12},{1,17},{... | collective-permute-start | bytes 884744 | tf_op jit(solution)/shard_map/ppermute | solution.py:443
  40.8 24.7 %collective-permute-start.17 = (bf16[384,768]{1,0:T(8,128)(2,1)}, bf16[384,768]{1,0:T(8,128)(2,1)}, u32[]{:S(2)}, u32[]{:S(2)}) collective-permute-start(bf16[384,768]{1,0:T(8,128)(2,1)} %param.22), channel_id=1, source_target_pairs={{0,16},{4,20},{8,24},{12,28},{16,0},{20,4},{24,8},{28,12},{1,17},{... | collective-permute-start | bytes 1769480 | tf_op jit(solution)/shard_map/ppermute | solution.py:443
  42.1 23.5 %collective-permute-start.15 = (bf16[144,3072]{1,0:T(8,128)(2,1)}, bf16[144,3072]{1,0:T(8,128)(2,1)S(1)}, u32[]{:S(2)}, u32[]{:S(2)}) collective-permute-start(bf16[144,3072]{1,0:T(8,128)(2,1)} %pad_maximum_fusion.4), channel_id=1, source_target_pairs={{0,8},{4,12},{8,0},{12,4},{16,24},{20,28},{24,16},{28,20},{1,9},{5... | collective-permute-start | bytes 2654216 | tf_op jit(solution)/shard_map/ppermute | solution.py:443
  83.0 25.7 %collective-permute-start.29 = (bf16[2,96,3072]{2,1,0:T(8,128)(2,1)S(1)}, bf16[2,96,3072]{2,1,0:T(8,128)(2,1)}, u32[]{:S(2)}, u32[]{:S(2)}) collective-permute-start(bf16[2,96,3072]{2,1,0:T(8,128)(2,1)S(1)} %pad_maximum_fusion.1.refs_4_), channel_id=1, source_target_pairs={{0,16},{4,20},{8,24},{12,28},{16,0},{20,4},{24,8},{28,12},{1,17},{... | collective-permute-start | bytes 3538952 | tf_op jit(solution)/shard_map/ppermute | solution.py:443
  83.8 25.5 %collective-permute-start.31 = (bf16[2,384,768]{2,1,0:T(8,128)(2,1)S(1)}, bf16[2,384,768]{2,1,0:T(8,128)(2,1)}, u32[]{:S(2)}, u32[]{:S(2)}) collective-permute-start(bf16[2,384,768]{2,1,0:T(8,128)(2,1)S(1)} %pad_maximum_fusion.2.refs_8_), channel_id=1, source_target_pairs={{0,8},{4,12},{8,0},{12,4},{16,24},{20,28},{24,16},{28,20},{1,9},{5... | collective-permute-start | bytes 3538952 | tf_op jit(solution)/shard_map/ppermute | solution.py:443
  103.7 24.8 %collective-permute-start.27 = (bf16[2,96,3072]{2,1,0:T(8,128)(2,1)S(1)}, bf16[2,96,3072]{2,1,0:T(8,128)(2,1)}, u32[]{:S(2)}, u32[]{:S(2)}) collective-permute-start(bf16[2,96,3072]{2,1,0:T(8,128)(2,1)S(1)} %pad_maximum_fusion.1.refs_4_), channel_id=1, source_target_pairs={{0,4},{4,0},{8,12},{12,8},{16,20},{20,16},{24,28},{28,24},{1,5},{5... | collective-permute-start | bytes 3538952 | tf_op jit(solution)/shard_map/ppermute | solution.py:443
  104.2 24.3 %collective-permute-start.28 = (bf16[2,384,768]{2,1,0:T(8,128)(2,1)S(1)}, bf16[2,384,768]{2,1,0:T(8,128)(2,1)}, u32[]{:S(2)}, u32[]{:S(2)}) collective-permute-start(bf16[2,384,768]{2,1,0:T(8,128)(2,1)S(1)} %pad_maximum_fusion.2.refs_8_), channel_id=1, source_target_pairs={{0,4},{4,0},{8,12},{12,8},{16,20},{20,16},{24,28},{28,24},{1,5},{5... | collective-permute-start | bytes 3538952 | tf_op jit(solution)/shard_map/ppermute | solution.py:443
  162.6 34.6 %collective-permute-start.41 = (bf16[2,96,3072]{2,1,0:T(8,128)(2,1)S(1)}, bf16[2,96,3072]{2,1,0:T(8,128)(2,1)}, u32[]{:S(2)}, u32[]{:S(2)}) collective-permute-start(bf16[2,96,3072]{2,1,0:T(8,128)(2,1)S(1)} %add_convert_fusion.1), channel_id=1, source_target_pairs={{0,8},{4,12},{8,0},{12,4},{16,24},{20,28},{24,16},{28,20},{1,9},{5... | collective-permute-start | bytes 3538952 | tf_op jit(solution)/shard_map/ppermute | solution.py:443
  164.5 35.1 %collective-permute-start.42 = (bf16[2,384,768]{2,1,0:T(8,128)(2,1)}, bf16[2,384,768]{2,1,0:T(8,128)(2,1)}, u32[]{:S(2)}, u32[]{:S(2)}) collective-permute-start(bf16[2,384,768]{2,1,0:T(8,128)(2,1)} %add_convert_fusion), channel_id=1, source_target_pairs={{0,16},{4,20},{8,24},{12,28},{16,0},{20,4},{24,8},{28,12},{1,17},{... | collective-permute-start | bytes 3538952 | tf_op jit(solution)/shard_map/ppermute | solution.py:443
  165.5 27.2 %collective-permute-start.35 = (bf16[2,49,768]{2,1,0:T(8,128)(2,1)}, bf16[2,49,768]{2,1,0:T(8,128)(2,1)S(1)}, u32[]{:S(2)}, u32[]{:S(2)}) collective-permute-start(bf16[2,49,768]{2,1,0:T(8,128)(2,1)} %get-tuple-element.230), channel_id=1, source_target_pairs={{0,1},{1,0},{2,3},{3,2},{4,5},{5,4},{6,7},{7,6},{8,9},{9,8},{10,11... | collective-permute-start | bytes 451592 | tf_op jit(solution)/shard_map/ppermute | solution.py:443
  165.5 27.3 %collective-permute-start.36 = (bf16[2,49,768]{2,1,0:T(8,128)(2,1)}, bf16[2,49,768]{2,1,0:T(8,128)(2,1)}, u32[]{:S(2)}, u32[]{:S(2)}) collective-permute-start(bf16[2,49,768]{2,1,0:T(8,128)(2,1)} %get-tuple-element.231), channel_id=1, source_target_pairs={{0,2},{1,3},{2,0},{3,1},{4,6},{5,7},{6,4},{7,5},{8,10},{9,11},{10,... | collective-permute-start | bytes 451592 | tf_op jit(solution)/shard_map/ppermute | solution.py:443
  166.4 26.3 %collective-permute-start.37 = (bf16[2,49,768]{2,1,0:T(8,128)(2,1)}, bf16[2,49,768]{2,1,0:T(8,128)(2,1)}, u32[]{:S(2)}, u32[]{:S(2)}) collective-permute-start(bf16[2,49,768]{2,1,0:T(8,128)(2,1)} %get-tuple-element.232), channel_id=1, source_target_pairs={{0,3},{1,2},{2,1},{3,0},{4,7},{5,6},{6,5},{7,4},{8,11},{9,10},{10,... | collective-permute-start | bytes 451592 | tf_op jit(solution)/shard_map/ppermute | solution.py:443
  208.3 25.2 %collective-permute-start.46 = (bf16[96,3072]{1,0:T(8,128)(2,1)}, bf16[96,3072]{1,0:T(8,128)(2,1)}, u32[]{:S(2)}, u32[]{:S(2)}) collective-permute-start(bf16[96,3072]{1,0:T(8,128)(2,1)} %fusion.3), channel_id=1, source_target_pairs={{0,16},{4,20},{8,24},{12,28},{16,0},{20,4},{24,8},{28,12},{1,17},{... | collective-permute-start | bytes 1769480 | tf_op jit(solution)/shard_map/ppermute | solution.py:443
  209.4 24.0 %collective-permute-start.47 = (bf16[384,768]{1,0:T(8,128)(2,1)}, bf16[384,768]{1,0:T(8,128)(2,1)}, u32[]{:S(2)}, u32[]{:S(2)}) collective-permute-start(bf16[384,768]{1,0:T(8,128)(2,1)} %fusion.4), channel_id=1, source_target_pairs={{0,8},{4,12},{8,0},{12,4},{16,24},{20,28},{24,16},{28,20},{1,9},{5... | collective-permute-start | bytes 1769480 | tf_op jit(solution)/shard_map/ppermute | solution.py:443
  214.6 23.1 %collective-permute-start.44 = (bf16[2,48,3072]{2,1,0:T(8,128)(2,1)}, bf16[2,48,3072]{2,1,0:T(8,128)(2,1)S(1)}, u32[]{:S(2)}, u32[]{:S(2)}) collective-permute-start(bf16[2,48,3072]{2,1,0:T(8,128)(2,1)} %get-tuple-element.261), channel_id=1, source_target_pairs={{0,8},{4,12},{8,0},{12,4},{16,24},{20,28},{24,16},{28,20},{1,9},{5... | collective-permute-start | bytes 1769480 | tf_op jit(solution)/shard_map/ppermute | solution.py:443
  214.8 22.9 %collective-permute-start.45 = (bf16[2,48,3072]{2,1,0:T(8,128)(2,1)}, bf16[2,48,3072]{2,1,0:T(8,128)(2,1)S(1)}, u32[]{:S(2)}, u32[]{:S(2)}) collective-permute-start(bf16[2,48,3072]{2,1,0:T(8,128)(2,1)} %get-tuple-element.262), channel_id=1, source_target_pairs={{0,16},{4,20},{8,24},{12,28},{16,0},{20,4},{24,8},{28,12},{1,17},{... | collective-permute-start | bytes 1769480 | tf_op jit(solution)/shard_map/ppermute | solution.py:443
  266.2 34.0 %collective-permute-start.57 = (bf16[96,3072]{1,0:T(8,128)(2,1)S(1)}, bf16[96,3072]{1,0:T(8,128)(2,1)S(1)}, u32[]{:S(2)}, u32[]{:S(2)}) collective-permute-start(bf16[96,3072]{1,0:T(8,128)(2,1)S(1)} %add_convert_fusion.3), channel_id=1, source_target_pairs={{0,2},{1,3},{2,0},{3,1},{4,6},{5,7},{6,4},{7,5},{8,10},{9,11},{10,... | collective-permute-start | bytes 1769480 | tf_op jit(solution)/shard_map/ppermute | solution.py:443
  279.1 21.3 %collective-permute-start.55 = (bf16[48,3072]{1,0:T(8,128)(2,1)S(1)}, bf16[48,3072]{1,0:T(8,128)(2,1)S(1)}, u32[]{:S(2)}, u32[]{:S(2)}) collective-permute-start(bf16[48,3072]{1,0:T(8,128)(2,1)S(1)} %get-tuple-element.324), channel_id=1, source_target_pairs={{0,8},{4,12},{8,0},{12,4},{16,24},{20,28},{24,16},{28,20},{1,9},{5... | collective-permute-start | bytes 884744 | tf_op jit(solution)/shard_map/ppermute | solution.py:443
  306.3 22.4 %collective-permute-start.63 = (bf16[48,3072]{1,0:T(8,128)(2,1)S(1)}, bf16[48,3072]{1,0:T(8,128)(2,1)S(1)}, u32[]{:S(2)}, u32[]{:S(2)}) collective-permute-start(bf16[48,3072]{1,0:T(8,128)(2,1)S(1)} %add_convert_fusion.13), channel_id=1, source_target_pairs={{0,2},{1,3},{2,0},{3,1},{4,6},{5,7},{6,4},{7,5},{8,10},{9,11},{10,... | collective-permute-start | bytes 884744 | tf_op jit(solution)/shard_map/ppermute | solution.py:443
  334.6 28.1 %collective-permute-start.68 = (bf16[96,3072]{1,0:T(8,128)(2,1)S(1)}, bf16[96,3072]{1,0:T(8,128)(2,1)S(1)}, u32[]{:S(2)}, u32[]{:S(2)}) collective-permute-start(bf16[96,3072]{1,0:T(8,128)(2,1)S(1)} %add_convert_fusion.2), channel_id=1, source_target_pairs={{0,1},{1,0},{2,3},{3,2},{4,5},{5,4},{6,7},{7,6},{8,9},{9,8},{10,11... | collective-permute-start | bytes 1769480 | tf_op jit(solution)/shard_map/ppermute | solution.py:443
  336.5 26.0 %collective-permute-start.66 = (bf16[48,3072]{1,0:T(8,128)(2,1)S(1)}, bf16[48,3072]{1,0:T(8,128)(2,1)S(1)}, u32[]{:S(2)}, u32[]{:S(2)}) collective-permute-start(bf16[48,3072]{1,0:T(8,128)(2,1)S(1)} %add_convert_fusion.11), channel_id=1, source_target_pairs={{0,1},{1,0},{2,3},{3,2},{4,5},{5,4},{6,7},{7,6},{8,9},{9,8},{10,11... | collective-permute-start | bytes 884744 | tf_op jit(solution)/shard_map/ppermute | solution.py:443
  336.6 25.7 %collective-permute-start.67 = (bf16[48,3072]{1,0:T(8,128)(2,1)S(1)}, bf16[48,3072]{1,0:T(8,128)(2,1)S(1)}, u32[]{:S(2)}, u32[]{:S(2)}) collective-permute-start(bf16[48,3072]{1,0:T(8,128)(2,1)S(1)} %add_convert_fusion.10), channel_id=1, source_target_pairs={{0,1},{1,0},{2,3},{3,2},{4,5},{5,4},{6,7},{7,6},{8,9},{9,8},{10,11... | collective-permute-start | bytes 884744 | tf_op jit(solution)/shard_map/ppermute | solution.py:443
  (107 other events, 1071.2 us)
